TPU v7x, 256 devices: a whole 4x4x8 slice. The times are simulated.
256 devices in a mesh: layer: 2 (over core), row: 32 (over x, z), col: 4 (over y).
Axes of the slice: x: 4, y: 4, z: 8, core: 2. Of those that a mesh axis runs over, the one named last changes fastest.
Arguments:
- tile_values: bfloat16 [2, 32, 4, 256, 128, 128], P('layer', 'row', 'col'), may hold values from -0.5 to 0.5
- tile_rows: int32 [2, 32, 4, 256], P('layer', 'row', 'col'), may hold values from 0 to 31
- tile_cols: int32 [2, 32, 4, 256], P('layer', 'row', 'col'), may hold values from 0 to 63
- tile_count: int32 [2, 32, 4], P('layer', 'row', 'col'), may hold values from 64 to 256, as said below
- start_panel: bfloat16 [32768, 128], P('col'), may hold values from -6 to 6
Outputs:
- caller_panel: bfloat16 [32, 4096, 128], P('row', ('layer', 'col'))
- dest_panel: bfloat16 [4, 8192, 128], P('col', ('layer', 'row'))
Inputs may be any that keep to these rules, and one draw needn't show every extreme that they name: tile_count reaches 256 on some device.
All inputs are finite; a program needn't handle non-finite values.
Results may differ from a plain program's by a relative error of at most 0.0049.
Values may be sent and summed in bfloat16 or wider, within the bound.
No kernel may reach another device: no remote copies, remote signals or barrier semaphores. Data moves between devices by JAX's collectives and lax.ppermute only.
A program may use at most 128 MiB of HBM per device.

v0:
```python
import jax
import jax.numpy as jnp
from jax import lax
from jax.sharding import PartitionSpec as P

TILE = 128
RANK = 128
CTILES = 32
DTILES = 64


EPS = 1e-06


def collect(prods, targets, groups):
    onehot = (targets[None, :] == jnp.arange(groups, dtype=jnp.int32)[:, None]).astype(jnp.float32)
    flat = prods.reshape(prods.shape[0], TILE * RANK)
    sums = jnp.dot(
        onehot, flat, precision=lax.Precision.HIGHEST, preferred_element_type=jnp.float32
    )
    return sums.reshape(groups * TILE, RANK)


def forward_tiles(tiles, rows, cols, panel):
    blocks = panel.reshape(-1, TILE, RANK)
    picked = jnp.take(blocks, cols, axis=0)
    prods = jnp.einsum("tij,tjr->tir", tiles, picked, preferred_element_type=jnp.float32)
    return collect(prods, rows, CTILES)


def backward_tiles(tiles, rows, cols, panel):
    blocks = panel.reshape(-1, TILE, RANK)
    picked = jnp.take(blocks, rows, axis=0)
    prods = jnp.einsum("tij,tir->tjr", tiles, picked, preferred_element_type=jnp.float32)
    return collect(prods, cols, DTILES)


def on_device(tile_values, tile_rows, tile_cols, tile_count, start_panel):
    tiles = tile_values[0, 0, 0]
    rows = tile_rows[0, 0, 0]
    cols = tile_cols[0, 0, 0]
    count = tile_count[0, 0, 0]
    live = jnp.arange(tiles.shape[0]) < count
    tiles = jnp.where(live[:, None, None], tiles, jnp.zeros((), jnp.bfloat16))
    n_layer = lax.axis_size("layer")
    n_row = lax.axis_size("row")
    n_col = lax.axis_size("col")
    caller_terms = forward_tiles(tiles, rows, cols, start_panel)
    summed = lax.psum(caller_terms, ("layer", "col"))
    caller_rounded = summed.astype(jnp.bfloat16)
    dest_terms = backward_tiles(tiles, rows, cols, caller_rounded)
    share = lax.psum_scatter(dest_terms, ("layer", "row"), scatter_dimension=0, tiled=True)
    squares = lax.psum(jnp.sum(share * share, axis=0), ("layer", "row", "col"))
    scale = lax.rsqrt(squares / (share.shape[0] * n_layer * n_row * n_col) + EPS)
    own_share = (share * scale).astype(jnp.bfloat16)
    dest_whole = lax.all_gather(own_share, ("layer", "row"), axis=0, tiled=True)
    last_terms = forward_tiles(tiles, rows, cols, dest_whole)
    last_share = lax.psum_scatter(last_terms, ("layer", "col"), scatter_dimension=0, tiled=True)
    return (last_share.astype(jnp.bfloat16)[None], own_share[None])


def solution(mesh):
    placed = (
        P("layer", "row", "col", None, None, None),
        P("layer", "row", "col", None),
        P("layer", "row", "col", None),
        P("layer", "row", "col"),
        P("col", None),
    )
    return jax.shard_map(
        on_device,
        mesh=mesh,
        in_specs=placed,
        out_specs=(P("row", ("layer", "col"), None), P("col", ("layer", "row"), None)),
        check_vma=False,
    )
```

profile of v0, /device:TPU:1, one launch (start us, length us, event | category | flops | bytes accessed | tf_op | source)
XLA Modules:
  0.0 538.9 jit_solution(9979345268950718430)
XLA Ops:
  8.0 0.7 compare_select_fusion
  8.7 0.7 compare_and_fusion.1
  9.4 0.7 compare_select_fusion.1
  10.1 0.7 compare_and_fusion
  10.8 8.6 %gather_fusion.1 = bf16[256,128,128]{2,1,0:T(8,128)(2,1)} fusion(bf16[64,128,128]{2,1,0:T(8,128)(2,1)S(1)} %bitcast.31, s32[1024]{0:T(1024)S(1)} %pad_clamp_fusion.1), kind=kCustom, calls=%fused_computation.clone | custom fusion | bytes 16778240 | tf_op jit(solution)/shard_map/jit(_take)/gather | solution.py:26
  19.4 10.5 %fusion.11 = f32[256,128,128]{2,1,0:T(8,128)} fusion(bf16[256,128,128]{2,1,0:T(8,128)(2,1)} %gather_fusion.1, pred[256]{0:T(512)(128)(4,1)S(1)} %get-tuple-element.3, bf16[1,1,1,256,128,128]{5,4,3,2,1,0:T(8,128)(2,1)} %param.7, pred[256]{0:T(512)(128)(4,1)S(1)} %get-tuple-element.4), kind=kOutput, calls=%fused_computation.15 | convolution fusion | flops 1082130432 | bytes 33554944 | tf_op jit(solution)/shard_map/tij,tjr->tir/dot_general | solution.py:27
  29.9 20.3 %fusion.6 = f32[32,16384]{1,0:T(8,128)S(1)} fusion(f32[32,8,128,128]{3,2,1,0:T(8,128)} %bitcast.34, s32[256]{0:T(256)S(1)} %bitcast.38), kind=kOutput, calls=%fused_computation.9 | convolution fusion | flops 1610620928 | bytes 18875392 | tf_op jit(solution)/shard_map/dot_general | solution.py:18
  50.3 1.5 reshape.79
  51.8 65.1 %all-reduce.1 = bf16[4096,128]{1,0:T(8,128)(2,1)S(1)} all-reduce(f32[4096,128]{1,0:T(8,128)} %reshape.79), channel_id=1, replica_groups=mesh['layer'=2,'row'=32,'col'=4] {'layer','col'}, use_global_device_ids=true, to_apply=%region_0.2 | all-reduce | flops 524288 | bytes 3145728 | tf_op jit(solution)/shard_map/psum | solution.py:49
  116.9 8.5 %gather_fusion = bf16[256,128,128]{2,1,0:T(8,128)(2,1)} fusion(bf16[32,128,128]{2,1,0:T(8,128)(2,1)S(1)} %bitcast.35, s32[1024]{0:T(1024)S(1)} %pad_clamp_fusion), kind=kCustom, calls=%fused_computation.2 | custom fusion | bytes 16778240 | tf_op jit(solution)/shard_map/jit(_take)/gather | solution.py:33
  125.4 11.3 %fusion.13 = f32[256,128,128]{2,1,0:T(8,128)} fusion(bf16[256,128,128]{2,1,0:T(8,128)(2,1)} %gather_fusion, pred[256]{0:T(512)(128)(4,1)S(1)} %compare_and_fusion.1, bf16[1,1,1,256,128,128]{5,4,3,2,1,0:T(8,128)(2,1)} %param.7, pred[256]{0:T(512)(128)(4,1)S(1)} %get-tuple-element.4), kind=kOutput, calls=%fused_computation.17 | convolution fusion | flops 1082130432 | bytes 33554944 | tf_op jit(solution)/shard_map/tij,tir->tjr/dot_general | solution.py:34
  136.7 15.7 %fusion.3 = f32[64,16384]{1,0:T(8,128)} fusion(f32[32,8,128,128]{3,2,1,0:T(8,128)} %bitcast.32, s32[256]{0:T(256)S(1)} %bitcast.42), kind=kOutput, calls=%fused_computation.6 | convolution fusion | flops 3221241856 | bytes 20972544 | tf_op jit(solution)/shard_map/dot_general | solution.py:18
  152.5 4.9 reshape.82
  157.4 140.9 %reduce-scatter.3.cloned.1.call-done = f32[128,128]{1,0:T(8,128)} async-done(((f32[8192,128]{1,0:T(8,128)}), f32[128,128]{1,0:T(8,128)}) %reduce-scatter.3.cloned.1.call-update) | async-done | bytes 65552 | tf_op jit(solution)/shard_map/reduce_scatter | solution.py:52
  298.3 0.9 multiply_reduce_fusion
  299.2 79.6 %psum.15 = f32[128]{0:T(128)S(1)} all-reduce(f32[128]{0:T(128)S(1)} %multiply_reduce_fusion), channel_id=1, replica_groups=mesh['layer'=2,'row'=32,'col'=4] {'layer','row','col'}, use_global_device_ids=true, to_apply=%region_3.5 | all-reduce | flops 128 | bytes 1024 | tf_op jit(solution)/shard_map/psum | solution.py:53
  378.7 1.5 multiply_convert_fusion
  380.3 74.2 %all-gather.2.cloned.1.call-done = bf16[8192,128]{1,0:T(8,128)(2,1)} async-done(((bf16[128,128]{1,0:T(8,128)(2,1)}), bf16[8192,128]{1,0:T(8,128)(2,1)}) %all-gather.2.cloned.1.call-update) | async-done | bytes 2097168 | tf_op jit(solution)/shard_map/all_gather | solution.py:56
  454.5 10.4 %gather_fusion.2 = bf16[256,128,128]{2,1,0:T(8,128)(2,1)} fusion(bf16[64,128,128]{2,1,0:T(8,128)(2,1)} %bitcast.36, s32[1024]{0:T(1024)S(1)} %pad_clamp_fusion.1), kind=kCustom, calls=%fused_computation.1.clone | custom fusion | bytes 16778240 | tf_op jit(solution)/shard_map/jit(_take)/gather | solution.py:26
  464.9 10.5 %fusion.9 = f32[256,128,128]{2,1,0:T(8,128)} fusion(bf16[256,128,128]{2,1,0:T(8,128)(2,1)} %gather_fusion.2, pred[256]{0:T(512)(128)(4,1)S(1)} %get-tuple-element.3, bf16[1,1,1,256,128,128]{5,4,3,2,1,0:T(8,128)(2,1)} %param.7, pred[256]{0:T(512)(128)(4,1)S(1)} %get-tuple-element.4), kind=kOutput, calls=%fused_computation.13 | convolution fusion | flops 1082130432 | bytes 33554944 | tf_op jit(solution)/shard_map/tij,tjr->tir/dot_general | solution.py:27
  475.5 14.7 %fusion = f32[32,16384]{1,0:T(8,128)} fusion(f32[32,8,128,128]{3,2,1,0:T(8,128)} %bitcast.33, s32[256]{0:T(256)S(1)} %bitcast.39), kind=kOutput, calls=%fused_computation.3 | convolution fusion | flops 1610620928 | bytes 18875392 | tf_op jit(solution)/shard_map/dot_general | solution.py:18
  490.1 2.7 reshape.85
  493.5 37.2 %reduce-scatter.5.cloned.1.call-done = f32[512,128]{1,0:T(8,128)} async-done(((f32[4096,128]{1,0:T(8,128)}), f32[512,128]{1,0:T(8,128)}) %reduce-scatter.5.cloned.1.call-update) | async-done | bytes 262160 | tf_op jit(solution)/shard_map/reduce_scatter | solution.py:58
  530.7 1.6 convert_bitcast_fusion
  (20 shorter events, 0.8 us)
Async XLA Ops:
  7.2 3.6 copy-start
  7.2 291.1 %reduce-scatter.3.cloned.1.call-start = ((), (), s32[]{:S(2)}) async-start(), calls=%async_computation.2 | async-start | bytes 4259840 | tf_op jit(solution)/shard_map/reduce_scatter | solution.py:52
  19.4 10.5 %copy-start.3 = (s32[1,1,1,256]{3,2,1,0:T(1,128)S(1)}, s32[1,1,1,256]{3,2,1,0:T(1,128)}, u32[]{:S(2)}) copy-start(s32[1,1,1,256]{3,2,1,0:T(1,128)} %param.8) | copy-start | bytes 3076
  125.4 11.3 %copy-start.4 = (s32[1,1,1,256]{3,2,1,0:T(1,128)S(1)}, s32[1,1,1,256]{3,2,1,0:T(1,128)}, u32[]{:S(2)}) copy-start(s32[1,1,1,256]{3,2,1,0:T(1,128)} %param.9) | copy-start | bytes 3076
  157.4 297.1 %all-gather.2.cloned.1.call-start = ((), (), s32[]{:S(2)}) async-start(), calls=%async_computation.3 | async-start | bytes 2129920 | tf_op jit(solution)/shard_map/all_gather | solution.py:56
  380.2 150.5 %reduce-scatter.5.cloned.1.call-start = ((), (), s32[]{:S(2)}) async-start(), calls=%async_computation.4 | async-start | bytes 2359296 | tf_op jit(solution)/shard_map/reduce_scatter | solution.py:58
  475.5 56.9 %copy-start.1 = (bf16[8192,128]{1,0:T(8,128)(2,1)S(1)}, bf16[8192,128]{1,0:T(8,128)(2,1)}, u32[]{:S(2)}) copy-start(bf16[8192,128]{1,0:T(8,128)(2,1)} %param.11) | copy-start | bytes 6291460
  475.5 17.4 %copy-start.2 = (f32[128,128]{1,0:T(8,128)S(1)}, f32[128,128]{1,0:T(8,128)}, u32[]{:S(2)}) copy-start(f32[128,128]{1,0:T(8,128)} %reduce-scatter.3.cloned.1.call-done) | copy-start | bytes 196612
Sparse Core Ops, SparseCore 0:
  157.5 140.8 reduce-scatter.2
  380.4 74.0 all-gather.1
  493.0 37.6 reduce-scatter.4
where the time goes:
time: 540 us; the launch traced here: 539 us
  waiting for transfers between devices  252 us (47%)
  blocking collectives  145 us (27%)
  matrix products  83.1 us (15%)
  local copies, waits for them, and re-layouts  36.8 us (7%)
  between operations  14.6 us (3%)
  other arithmetic  7.33 us (1%)
    reduce_scatter x1, waiting for transfers between devices, on_device(): lax.psum_scatter(dest_terms, ('layer', 'row'), scatter_dimension=0, tiled...  141 us
    psum x1, blocking collectives, on_device(): squares = lax.psum(jnp.sum(share * share, axis=0), ('layer', 'row', 'col'))  79.6 us
    all_gather x1, waiting for transfers between devices, on_device(): dest_whole = lax.all_gather(own_share, ('layer', 'row'), axis=0, tiled=True)  74.2 us
    psum x1, blocking collectives, on_device(): summed = lax.psum(caller_terms, ('layer', 'col'))  65.1 us
    dot_general x3, matrix products, collect(): jnp.dot(onehot, flat, precision=lax.Precision.HIGHEST, preferred_element_...  50.7 us
    reduce_scatter x1, waiting for transfers between devices, on_device(): lax.psum_scatter(last_terms, ('layer', 'col'), scatter_dimension=0, tiled...  37.2 us
    dot_general x2, matrix products, forward_tiles(): jnp.einsum('tij,tjr->tir', tiles, picked, preferred_element_type=jnp.floa...  21 us
    gather x2, local copies, waits for them, and re-layouts, forward_tiles(): picked = jnp.take(blocks, cols, axis=0)  19.1 us
  transfers between devices with their start and end apart: 3, of which 3 were waited for; matrix products, arithmetic and copies ran while one was open for 0% of the time, Pallas kernels for 0%

commit v1 on v0

v1 whole, which is shorter than its diff:
```python
import functools

import jax
import jax.numpy as jnp
from jax import lax
from jax.experimental import pallas as pl
from jax.experimental.pallas import tpu as pltpu
from jax.sharding import Mesh
from jax.sharding import PartitionSpec as P

TILE = 128
RANK = 128
CTILES = 32
DTILES = 64
NX = 4
NZ = 8
NCOL = 4
NDST = 32768
BLOCK = 64
UNROLL = 16
EPS = 1e-06

F32 = jnp.float32
BF16 = jnp.bfloat16
CORE, XPOS, ZPOS, COL = 0, 1, 2, 3

SMEM = pl.BlockSpec(memory_space=pltpu.SMEM)
VMEM = pl.BlockSpec(memory_space=pltpu.VMEM)
PARAMS = pltpu.CompilerParams(vmem_limit_bytes=40 * 2**20)


def tiles_of(n, dtype):
    return jax.ShapeDtypeStruct((n, TILE, RANK), dtype)


def each(n, body):
    def step(i, carry):
        body(i)
        return carry

    lax.fori_loop(0, n, step, 0)


def accumulate(step, dst, src, count, tiles_ref, panel, acc, dump, tile_left):
    live = count[0]
    left = jnp.minimum(live - step * BLOCK, BLOCK)

    def group(g, carry):
        for j in range(UNROLL):
            k = g * UNROLL + j
            t = step * BLOCK + k
            d = jnp.where(t < live, dst[t], dump)
            tile, block = tiles_ref[k], panel[src[t]]
            a, b = (tile, block) if tile_left else (block, tile)
            acc[d] += jnp.dot(a, b, preferred_element_type=F32)
        return carry

    lax.fori_loop(0, (left + UNROLL - 1) // UNROLL, group, 0)


def split(ids, acc, keep, send, half):
    core = ids[CORE]

    def one(i):
        keep[i] = acc[core * half + i]
        send[i] = acc[(1 - core) * half + i].astype(BF16)

    each(half, one)


def place(ids, parts, panel, axis, n, per, half):
    core, me = ids[CORE], ids[axis]
    for side in range(2):
        base = jnp.where(side == 0, core, 1 - core) * half
        for k in range(n):
            at = base + lax.rem(me + n - k, n) * per
            part = parts[side * n + k]

            def one(i):
                panel[at + i] = part[i]

            each(per, one)


def zero(acc):
    def one(i):
        acc[i] = jnp.zeros((TILE, RANK), F32)

    each(acc.shape[0], one)


def first_kernel(dst, src, count, ids, tiles_ref, panel, keep, send, acc):
    step = pl.program_id(0)

    @pl.when(step == 0)
    def _():
        zero(acc)

    accumulate(step, dst, src, count, tiles_ref, panel, acc, CTILES, True)

    @pl.when(step == pl.num_programs(0) - 1)
    def _():
        split(ids, acc, keep, send, CTILES // 2)


def back_kernel(dst, src, count, ids, tiles_ref, *refs):
    parts, (keep, send, panel, acc) = refs[: 2 * NCOL], refs[2 * NCOL :]
    step = pl.program_id(0)

    @pl.when(step == 0)
    def _():
        zero(acc)
        place(ids, parts, panel, COL, NCOL, CTILES // 2 // NCOL, CTILES // 2)

    accumulate(step, dst, src, count, tiles_ref, panel, acc, DTILES, False)

    @pl.when(step == pl.num_programs(0) - 1)
    def _():
        split(ids, acc, keep, send, DTILES // 2)


def last_kernel(dst, src, count, ids, tiles_ref, *refs):
    parts, (keep, send, squares, panel, acc) = refs[: 2 * NX], refs[2 * NX :]
    step = pl.program_id(0)

    @pl.when(step == 0)
    def _():
        zero(acc)
        place(ids, parts, panel, XPOS, NX, NZ, DTILES // 2)

    accumulate(step, dst, src, count, tiles_ref, panel, acc, CTILES, True)

    @pl.when(step == pl.num_programs(0) - 1)
    def _():
        split(ids, acc, keep, send, CTILES // 2)

        def one(i, total):
            block = panel[i].astype(F32)
            return total + jnp.sum((block * block).reshape(TILE // 8, 8, RANK), axis=0)

        squares[...] = lax.fori_loop(0, DTILES, one, jnp.zeros((8, RANK), F32))


def tile_pass(kernel, dst, src, count, ids, tiles, parts, n_acc, panel_tiles, extra, name):
    whole = lambda n: pl.BlockSpec((n, TILE, RANK), lambda i, *_: (0, 0, 0))
    half = n_acc // 2
    scratch = [pltpu.VMEM((n_acc + 1, TILE, RANK), F32)]
    if panel_tiles:
        scratch.insert(0, pltpu.VMEM((panel_tiles, TILE, RANK), BF16))
    return pl.pallas_call(
        kernel,
        grid_spec=pltpu.PrefetchScalarGridSpec(
            num_scalar_prefetch=4,
            grid=(tiles.shape[0] // BLOCK,),
            in_specs=[
                pl.BlockSpec(
                    (BLOCK, TILE, TILE),
                    lambda i, dst, src, count, ids: (jnp.minimum(i, (count[0] - 1) // BLOCK), 0, 0),
                )
            ]
            + [whole(p.shape[0]) for p in parts],
            out_specs=[whole(half), whole(half)]
            + [pl.BlockSpec(e.shape, lambda i, *_: (0, 0)) for e in extra],
            scratch_shapes=scratch,
        ),
        out_shape=[tiles_of(half, F32), tiles_of(half, BF16)] + extra,
        compiler_params=PARAMS,
        name=name,
    )(dst, src, count, ids, tiles, *parts)


def pair_kernel(ids, keep, got, own, *sends, axis, n, per):
    me = ids[axis]
    for k in range(n):
        base = lax.rem(me + k, n) * per

        def one(i):
            total = keep[base + i] + got[base + i].astype(F32)
            if k == 0:
                own[i] = total
            else:
                sends[k - 1][i] = total.astype(BF16)

        each(per, one)


def pair_sum(ids, keep, got, axis, n, per, name):
    return pl.pallas_call(
        functools.partial(pair_kernel, axis=axis, n=n, per=per),
        in_specs=[SMEM, VMEM, VMEM],
        out_specs=[VMEM] * n,
        out_shape=[tiles_of(per, F32)] + [tiles_of(per, BF16)] * (n - 1),
        compiler_params=PARAMS,
        name=name,
    )(ids, keep, got)


def caller_kernel(own, a, b, c, out):
    def one(i):
        total = own[i] + a[i].astype(F32) + b[i].astype(F32) + c[i].astype(F32)
        out[i] = total.astype(BF16).astype(F32).T.astype(BF16)

    each(own.shape[0], one)


def row_kernel(own, a, b, c, out):
    def one(i):
        total = own[i] + a[i].astype(F32) + b[i].astype(F32) + c[i].astype(F32)
        out[i] = total.astype(BF16)

    each(own.shape[0], one)


def four_sum(kernel, own, got, name):
    return pl.pallas_call(
        kernel,
        in_specs=[VMEM] * 4,
        out_specs=VMEM,
        out_shape=tiles_of(own.shape[0], BF16),
        compiler_params=PARAMS,
        name=name,
    )(own, *got)


def share_kernel(got, share, copies):
    total = got[0].astype(F32)
    for k in range(1, NZ):
        total += got[k].astype(F32)
    total = total.T
    share[...] = total
    for k in range(NZ):
        copies[k] = total.astype(BF16)


def last_pair_kernel(ids, keep, got, squares, own, *sends):
    me = ids[COL]
    per = CTILES // 2 // NCOL
    total = jnp.sum(squares[...], axis=0, keepdims=True)
    high = total.astype(BF16).astype(F32)
    middle = (total - high).astype(BF16).astype(F32)
    low = total - high - middle
    row = lax.broadcasted_iota(jnp.int32, (16, RANK), 0)
    coded = jnp.where(row == 0, high, jnp.where(row == 1, middle, jnp.where(row == 2, low, 0.0)))
    for k in range(NCOL):
        base = lax.rem(me + k, NCOL) * per
        if k:
            sends[k - 1][pl.ds(per * TILE, 16), :] = coded.astype(BF16)
        for i in range(per):
            part = keep[base + i] + got[base + i].astype(F32)
            if k == 0:
                own[i] = part
            else:
                sends[k - 1][pl.ds(i * TILE, TILE), :] = part.astype(BF16)


def final_kernel(own, squares, share, a, b, c, caller, dest):
    per = CTILES // 2 // NCOL
    total = jnp.sum(squares[...], axis=0, keepdims=True)
    for got in (a, b, c):
        total += jnp.sum(got[pl.ds(per * TILE, 16), :].astype(F32), axis=0, keepdims=True)
    scale = lax.rsqrt(total / NDST + EPS)
    dest[...] = (share[...] * scale).astype(BF16)
    for i in range(per):
        at = pl.ds(i * TILE, TILE)
        part = own[i] + a[at, :].astype(F32) + b[at, :].astype(F32) + c[at, :].astype(F32)
        caller[at, :] = (part * scale).astype(BF16)


def shifted(value, axis, k, n):
    return lax.ppermute(value, axis, [(i, (i + k) % n) for i in range(n)])


def swap(value):
    return lax.ppermute(value, "layer", [(0, 1), (1, 0)])


def exchange(values, axis, n):
    return [shifted(v, axis, k + 1, n) for k, v in enumerate(values)]


def gather(value, axis, n):
    mine = [value] + [shifted(value, axis, k, n) for k in range(1, n)]
    return mine + [swap(v) for v in mine]


def on_device(tile_values, tile_rows, tile_cols, tile_count, start_panel):
    tiles = tile_values[0, 0, 0]
    rows = tile_rows[0, 0, 0]
    cols = tile_cols[0, 0, 0]
    count = tile_count[0, 0]
    ids = jnp.stack([lax.axis_index(a) for a in ("layer", "x", "z", "col")]).astype(jnp.int32)
    start = start_panel.reshape(DTILES, TILE, RANK)
    quarter = CTILES // 2 // NCOL

    keep, send = tile_pass(first_kernel, rows, cols, count, ids, tiles, [start], CTILES, 0, [], "first_pass")
    own, *sends = pair_sum(ids, keep, swap(send), COL, NCOL, quarter, "first_pair")
    part = four_sum(caller_kernel, own, exchange(sends, "col", NCOL), "first_sum")
    parts = gather(part, "col", NCOL)

    keep, send = tile_pass(back_kernel, cols, rows, count, ids, tiles, parts, DTILES, CTILES, [], "back_pass")
    own, *sends = pair_sum(ids, keep, swap(send), XPOS, NX, NZ, "back_pair")
    part = four_sum(row_kernel, own, exchange(sends, "x", NX), "back_sum")
    got = lax.all_to_all(part, "z", split_axis=0, concat_axis=0, tiled=True)
    share, copies = pl.pallas_call(
        share_kernel,
        in_specs=[VMEM],
        out_specs=[VMEM, VMEM],
        out_shape=[jax.ShapeDtypeStruct((TILE, RANK), F32), tiles_of(NZ, BF16)],
        compiler_params=PARAMS,
        name="share_sum",
    )(got)
    part = lax.all_to_all(copies, "z", split_axis=0, concat_axis=0, tiled=True)
    parts = gather(part, "x", NX)

    keep, send, squares = tile_pass(
        last_kernel, rows, cols, count, ids, tiles, parts, CTILES, DTILES,
        [jax.ShapeDtypeStruct((8, RANK), F32)], "last_pass",
    )
    chunk = jax.ShapeDtypeStruct((quarter * TILE + 16, RANK), BF16)
    own, *sends = pl.pallas_call(
        last_pair_kernel,
        in_specs=[SMEM, VMEM, VMEM, VMEM],
        out_specs=[VMEM] * NCOL,
        out_shape=[tiles_of(quarter, F32)] + [chunk] * (NCOL - 1),
        compiler_params=PARAMS,
        name="last_pair",
    )(ids, keep, swap(send), squares)
    got = exchange(sends, "col", NCOL)
    caller, dest = pl.pallas_call(
        final_kernel,
        in_specs=[VMEM] * 6,
        out_specs=[VMEM, VMEM],
        out_shape=[
            jax.ShapeDtypeStruct((quarter * TILE, RANK), BF16),
            jax.ShapeDtypeStruct((TILE, RANK), BF16),
        ],
        compiler_params=PARAMS,
        name="final",
    )(own, squares, share, *got)
    return caller[None], dest[None]


def solution(mesh):
    fine = Mesh(mesh.devices.reshape(2, NX, NZ, NCOL), ("layer", "x", "z", "col"))
    row = ("x", "z")
    placed = (
        P("layer", row, "col", None, None, None),
        P("layer", row, "col", None),
        P("layer", row, "col", None),
        P("layer", row, "col"),
        P("col", None),
    )
    return jax.shard_map(
        on_device,
        mesh=fine,
        in_specs=placed,
        out_specs=(P(row, ("layer", "col"), None), P("col", ("layer", "x", "z"), None)),
        check_vma=False,
    )
```

time: 540 us -> 137 us (0.25)
  waiting for transfers between devices: 252 us -> 36.7 us
  blocking collectives: 145 us -> 31.4 us
  matrix products: 83.1 us -> 0 us
  starting transfers between devices: 0.12 us -> 41.4 us
  local copies, waits for them, and re-layouts: 36.8 us -> 6.35 us
  Pallas kernels: 0 us -> 18.6 us
  between operations: 14.6 us -> 1.42 us
  other arithmetic: 7.33 us -> 0.08 us
    reduce_scatter x2 -> x0, waiting for transfers between devices: 178 us -> none  [the longest x1 141 us: on_device(): lax.psum_scatter(dest_terms, ('layer', 'row'), scatter_dimension=0, tiled...]
    psum x2 -> x0, blocking collectives: 145 us -> none  [the longest x1 79.6 us: on_device(): squares = lax.psum(jnp.sum(share * share, axis=0), ('layer', 'row', 'col'))]
    dot_general x6 -> x0, matrix products: 83.1 us -> none  [the longest x3 50.7 us: collect(): jnp.dot(onehot, flat, precision=lax.Precision.HIGHEST, preferred_element_...]
    all_gather x1 -> x0, waiting for transfers between devices: 74.2 us -> none  [on_device(): dest_whole = lax.all_gather(own_share, ('layer', 'row'), axis=0, tiled=True)]
    ppermute x0 -> x26, starting transfers between devices: none -> 41.4 us  [the longest x11 22.2 us: swap(): return lax.ppermute(value, 'layer', [(0, 1), (1, 0)])]
    ppermute x0 -> x26, waiting for transfers between devices: none -> 36.7 us  [the longest x15 28.5 us: shifted(): return lax.ppermute(value, axis, [(i, (i + k) % n) for i in range(n)])]
    all_to_all x0 -> x2, blocking collectives: none -> 31.4 us  [the longest x1 19.5 us: on_device(): got = lax.all_to_all(part, 'z', split_axis=0, concat_axis=0, tiled=True)]
    gather x3 -> x0, local copies, waits for them, and re-layouts: 27.6 us -> none  [the longest x2 19.1 us: forward_tiles(): picked = jnp.take(blocks, cols, axis=0)]
  transfers between devices with their start and end apart: 3 -> 26, of which waited for: 3 -> 16; matrix products, arithmetic and copies ran while one was open for 0% -> 0% of each run, Pallas kernels for 0% -> 0%
where the time goes in v1:
time: 137 us; the launch traced here: 136 us
  starting transfers between devices  41.4 us (30%)
  waiting for transfers between devices  36.7 us (27%)
  blocking collectives  31.4 us (23%)
  Pallas kernels  18.6 us (14%)
  local copies, waits for them, and re-layouts  6.35 us (5%)
  between operations  1.42 us (1%)
    ppermute x15, waiting for transfers between devices, shifted(): return lax.ppermute(value, axis, [(i, (i + k) % n) for i in range(n)])  28.5 us
    ppermute x11, starting transfers between devices, swap(): return lax.ppermute(value, 'layer', [(0, 1), (1, 0)])  22.2 us
    all_to_all x1, blocking collectives, on_device(): got = lax.all_to_all(part, 'z', split_axis=0, concat_axis=0, tiled=True)  19.5 us
    ppermute x15, starting transfers between devices, shifted(): return lax.ppermute(value, axis, [(i, (i + k) % n) for i in range(n)])  19.1 us
    pallas_call x3, Pallas kernels, tile_pass(): pl.pallas_call(kernel, grid_spec=pltpu.PrefetchScalarGridSpec(num_scalar_...  14.9 us
    all_to_all x1, blocking collectives, on_device(): part = lax.all_to_all(copies, 'z', split_axis=0, concat_axis=0, tiled=True)  11.9 us
    ppermute x11, waiting for transfers between devices, swap(): return lax.ppermute(value, 'layer', [(0, 1), (1, 0)])  8.22 us
    unnamed x14, local copies, waits for them, and re-layouts  6.35 us
  transfers between devices with their start and end apart: 26, of which 16 were waited for; matrix products, arithmetic and copies ran while one was open for 0% of the time, Pallas kernels for 0%

profile of v1, /device:TPU:1, one launch (start us, length us, event | category | flops | bytes accessed | tf_op | source)
XLA Modules:
  0.0 136.0 jit_solution(9201208708712557147)
XLA Ops:
  1.4 3.4 %copy-done = bf16[1,1,1,256,128,128]{5,4,3,2,1,0:T(8,128)(2,1)S(1)} copy-done((bf16[1,1,1,256,128,128]{5,4,3,2,1,0:T(8,128)(2,1)S(1)}, bf16[1,1,1,256,128,128]{5,4,3,2,1,0:T(8,128)(2,1)}, u32[]{:S(2)}) %copy-start) | copy-done | bytes 8388632
  7.7 4.2 %first_pass.1 = (f32[16,128,128]{2,1,0:T(8,128)S(1)}, bf16[16,128,128]{2,1,0:T(8,128)(2,1)S(1)}) custom-call(s32[256]{0:T(256)S(1)} %bitcast.18, s32[256]{0:T(256)S(1)} %bitcast.21, s32[1]{0:T(128)} %bitcast.11.count, s32[4]{0:T(128)S(1)} %pad_add_fusion.ids, bf16[256,128,128]{2,1,0:T(8,128)(2,1)S(1)} %bitcast.14, bf16[64,128,128]{2,1,0:T(8,128)(2,1)S(1)} %bitcast.17), custom_call_target="tpu_custom_call" | custom-call | tf_op jit(solution)/shard_map/first_pass/pallas_call | solution.py:150
  11.9 2.1 %collective-permute-start = (bf16[16,128,128]{2,1,0:T(8,128)(2,1)S(1)}, bf16[16,128,128]{2,1,0:T(8,128)(2,1)S(1)}, u32[]{:S(2)}, u32[]{:S(2)}) collective-permute-start(bf16[16,128,128]{2,1,0:T(8,128)(2,1)S(1)} %get-tuple-element.26), channel_id=1, source_target_pairs={{0,128},{128,0},{1,129},{129,1},{2,130},{130,2},{3,131},{131,3},{4... | collective-permute-start | bytes 1572872 | tf_op jit(solution)/shard_map/ppermute | solution.py:274
  16.8 4.5 %collective-permute-start.2 = (bf16[4,128,128]{2,1,0:T(8,128)(2,1)S(1)}, bf16[4,128,128]{2,1,0:T(8,128)(2,1)S(1)}, u32[]{:S(2)}, u32[]{:S(2)}) collective-permute-start(bf16[4,128,128]{2,1,0:T(8,128)(2,1)S(1)} %get-tuple-element.29), channel_id=1, source_target_pairs={{0,2},{1,3},{2,0},{3,1},{4,6},{5,7},{6,4},{7,5},{8,10},{9,11},{10,... | collective-permute-start | bytes 393224 | tf_op jit(solution)/shard_map/ppermute | solution.py:270
  21.5 2.2 %collective-permute-done.1.a = bf16[4,128,128]{2,1,0:T(8,128)(2,1)S(1)} collective-permute-done((bf16[4,128,128]{2,1,0:T(8,128)(2,1)S(1)}, bf16[4,128,128]{2,1,0:T(8,128)(2,1)S(1)}, u32[]{:S(2)}, u32[]{:S(2)}) %collective-permute-start.1) | collective-permute-done | bytes 131104 | tf_op jit(solution)/shard_map/ppermute | solution.py:270
  23.7 3.7 %collective-permute-done.2.b = bf16[4,128,128]{2,1,0:T(8,128)(2,1)S(1)} collective-permute-done((bf16[4,128,128]{2,1,0:T(8,128)(2,1)S(1)}, bf16[4,128,128]{2,1,0:T(8,128)(2,1)S(1)}, u32[]{:S(2)}, u32[]{:S(2)}) %collective-permute-start.2) | collective-permute-done | bytes 131104 | tf_op jit(solution)/shard_map/ppermute | solution.py:270
  27.8 2.6 %collective-permute-start.6 = (bf16[4,128,128]{2,1,0:T(8,128)(2,1)S(1)}, bf16[4,128,128]{2,1,0:T(8,128)(2,1)S(1)}, u32[]{:S(2)}, u32[]{:S(2)}) collective-permute-start(bf16[4,128,128]{2,1,0:T(8,128)(2,1)S(1)} %first_sum.1.refs_0_), channel_id=1, source_target_pairs={{0,3},{1,0},{2,1},{3,2},{4,7},{5,4},{6,5},{7,6},{8,11},{9,8},{10,9... | collective-permute-start | bytes 393224 | tf_op jit(solution)/shard_map/ppermute | solution.py:270
  32.2 2.0 %collective-permute-done.6.refs_3_ = bf16[4,128,128]{2,1,0:T(8,128)(2,1)S(1)} collective-permute-done((bf16[4,128,128]{2,1,0:T(8,128)(2,1)S(1)}, bf16[4,128,128]{2,1,0:T(8,128)(2,1)S(1)}, u32[]{:S(2)}, u32[]{:S(2)}) %collective-permute-start.6) | collective-permute-done | bytes 131104 | tf_op jit(solution)/shard_map/ppermute | solution.py:270
  34.2 2.7 %collective-permute-start.10 = (bf16[4,128,128]{2,1,0:T(8,128)(2,1)S(1)}, bf16[4,128,128]{2,1,0:T(8,128)(2,1)S(1)}, u32[]{:S(2)}, u32[]{:S(2)}) collective-permute-start(bf16[4,128,128]{2,1,0:T(8,128)(2,1)S(1)} %collective-permute-done.6.refs_3_), channel_id=1, source_target_pairs={{0,128},{128,0},{1,129},{129,1},{2,130},{130,2},{3,131},{131,3},{4... | collective-permute-start | bytes 393224 | tf_op jit(solution)/shard_map/ppermute | solution.py:274
  37.0 2.2 %collective-permute-start.9 = (bf16[4,128,128]{2,1,0:T(8,128)(2,1)S(1)}, bf16[4,128,128]{2,1,0:T(8,128)(2,1)S(1)}, u32[]{:S(2)}, u32[]{:S(2)}) collective-permute-start(bf16[4,128,128]{2,1,0:T(8,128)(2,1)S(1)} %collective-permute-done.5.refs_2_), channel_id=1, source_target_pairs={{0,128},{128,0},{1,129},{129,1},{2,130},{130,2},{3,131},{131,3},{4... | collective-permute-start | bytes 393224 | tf_op jit(solution)/shard_map/ppermute | solution.py:274
  41.6 4.8 %back_pass.1 = (f32[32,128,128]{2,1,0:T(8,128)S(1)}, bf16[32,128,128]{2,1,0:T(8,128)(2,1)S(1)}) custom-call(s32[256]{0:T(256)S(1)} %bitcast.22, s32[256]{0:T(256)S(1)} %bitcast.19, s32[1]{0:T(128)} %bitcast.12.count, s32[4]{0:T(128)S(1)} %pad_add_fusion.ids, bf16[256,128,128]{2,1,0:T(8,128)(2,1)S(1)} %bitcast.15, bf16[4,128,128]{2,1,0:T(8,128)(2,1)S(1)} %first_sum.1.refs_0_, ...), custom_call_target="tpu_custom_call" | custom-call | tf_op jit(solution)/shard_map/back_pass/pallas_call | solution.py:150
  46.5 2.6 %collective-permute-done.11.got = bf16[32,128,128]{2,1,0:T(8,128)(2,1)S(1)} collective-permute-done((bf16[32,128,128]{2,1,0:T(8,128)(2,1)S(1)}, bf16[32,128,128]{2,1,0:T(8,128)(2,1)S(1)}, u32[]{:S(2)}, u32[]{:S(2)}) %collective-permute-start.11) | collective-permute-done | bytes 1048608 | tf_op jit(solution)/shard_map/ppermute | solution.py:274
  52.1 2.0 %collective-permute-start.14 = (bf16[8,128,128]{2,1,0:T(8,128)(2,1)S(1)}, bf16[8,128,128]{2,1,0:T(8,128)(2,1)S(1)}, u32[]{:S(2)}, u32[]{:S(2)}) collective-permute-start(bf16[8,128,128]{2,1,0:T(8,128)(2,1)S(1)} %get-tuple-element.36), channel_id=1, source_target_pairs={{0,96},{32,0},{64,32},{96,64},{1,97},{33,1},{65,33},{97,65},{2,98}... | collective-permute-start | bytes 786440 | tf_op jit(solution)/shard_map/ppermute | solution.py:270
  54.0 10.7 %collective-permute-done.12.a = bf16[8,128,128]{2,1,0:T(8,128)(2,1)S(1)} collective-permute-done((bf16[8,128,128]{2,1,0:T(8,128)(2,1)S(1)}, bf16[8,128,128]{2,1,0:T(8,128)(2,1)S(1)}, u32[]{:S(2)}, u32[]{:S(2)}) %collective-permute-start.12) | collective-permute-done | bytes 262176 | tf_op jit(solution)/shard_map/ppermute | solution.py:270
  65.2 19.5 %all_to_all.10.got = bf16[8,128,128]{2,1,0:T(8,128)(2,1)S(1)} all-to-all(bf16[8,128,128]{2,1,0:T(8,128)(2,1)S(1)} %back_sum.1), channel_id=1, replica_groups=mesh['layer'=2,'x'=4,'z'=8,'col'=4] {'z'}, dimensions={0} | all-to-all | bytes 524288 | tf_op jit(solution)/shard_map/all_to_all | solution.py:303
  84.8 11.9 %all_to_all.11.refs_0_ = bf16[8,128,128]{2,1,0:T(8,128)(2,1)S(1)} all-to-all(bf16[8,128,128]{2,1,0:T(8,128)(2,1)S(1)} %get-tuple-element.37), channel_id=1, replica_groups=mesh['layer'=2,'x'=4,'z'=8,'col'=4] {'z'}, dimensions={0} | all-to-all | bytes 524288 | tf_op jit(solution)/shard_map/all_to_all | solution.py:312
  96.7 3.4 %collective-permute-start.17 = (bf16[8,128,128]{2,1,0:T(8,128)(2,1)S(1)}, bf16[8,128,128]{2,1,0:T(8,128)(2,1)S(1)}, u32[]{:S(2)}, u32[]{:S(2)}) collective-permute-start(bf16[8,128,128]{2,1,0:T(8,128)(2,1)S(1)} %all_to_all.11.refs_0_), channel_id=1, source_target_pairs={{0,96},{32,0},{64,32},{96,64},{1,97},{33,1},{65,33},{97,65},{2,98}... | collective-permute-start | bytes 786440 | tf_op jit(solution)/shard_map/ppermute | solution.py:270
  100.7 4.1 %collective-permute-start.18 = (bf16[8,128,128]{2,1,0:T(8,128)(2,1)S(1)}, bf16[8,128,128]{2,1,0:T(8,128)(2,1)S(1)}, u32[]{:S(2)}, u32[]{:S(2)}) collective-permute-start(bf16[8,128,128]{2,1,0:T(8,128)(2,1)S(1)} %all_to_all.11.refs_0_), channel_id=1, source_target_pairs={{0,128},{128,0},{1,129},{129,1},{2,130},{130,2},{3,131},{131,3},{4... | collective-permute-start | bytes 786440 | tf_op jit(solution)/shard_map/ppermute | solution.py:274
  106.3 5.9 %collective-permute-start.21 = (bf16[8,128,128]{2,1,0:T(8,128)(2,1)S(1)}, bf16[8,128,128]{2,1,0:T(8,128)(2,1)S(1)}, u32[]{:S(2)}, u32[]{:S(2)}) collective-permute-start(bf16[8,128,128]{2,1,0:T(8,128)(2,1)S(1)} %collective-permute-done.17.refs_3_), channel_id=1, source_target_pairs={{0,128},{128,0},{1,129},{129,1},{2,130},{130,2},{3,131},{131,3},{4... | collective-permute-start | bytes 786440 | tf_op jit(solution)/shard_map/ppermute | solution.py:274
  113.8 2.2 %collective-permute-start.19 = (bf16[8,128,128]{2,1,0:T(8,128)(2,1)S(1)}, bf16[8,128,128]{2,1,0:T(8,128)(2,1)S(1)}, u32[]{:S(2)}, u32[]{:S(2)}) collective-permute-start(bf16[8,128,128]{2,1,0:T(8,128)(2,1)S(1)} %collective-permute-done.15.refs_1_), channel_id=1, source_target_pairs={{0,128},{128,0},{1,129},{129,1},{2,130},{130,2},{3,131},{131,3},{4... | collective-permute-start | bytes 786440 | tf_op jit(solution)/shard_map/ppermute | solution.py:274
  117.1 5.9 %last_pass.1 = (f32[16,128,128]{2,1,0:T(8,128)S(1)}, bf16[16,128,128]{2,1,0:T(8,128)(2,1)S(1)}, f32[8,128]{1,0:T(8,128)S(1)}) custom-call(s32[256]{0:T(256)S(1)} %bitcast.20, s32[256]{0:T(256)S(1)} %bitcast.23, s32[1]{0:T(128)} %bitcast.13.count, s32[4]{0:T(128)S(1)} %pad_add_fusion.ids, bf16[256,128,128]{2,1,0:T(8,128)(2,1)S(1)} %bitcast.16, ...), custom_call_target="tpu_custom_call" | custom-call | tf_op jit(solution)/shard_map/last_pass/pallas_call | solution.py:150
  125.8 2.6 %collective-permute-start.24 = (bf16[528,128]{1,0:T(8,128)(2,1)S(1)}, bf16[528,128]{1,0:T(8,128)(2,1)S(1)}, u32[]{:S(2)}, u32[]{:S(2)}) collective-permute-start(bf16[528,128]{1,0:T(8,128)(2,1)S(1)} %get-tuple-element.44), channel_id=1, source_target_pairs={{0,2},{1,3},{2,0},{3,1},{4,6},{5,7},{6,4},{7,5},{8,10},{9,11},{10,... | collective-permute-start | bytes 405512 | tf_op jit(solution)/shard_map/ppermute | solution.py:270
  128.5 3.9 %collective-permute-done.23.a = bf16[528,128]{1,0:T(8,128)(2,1)S(1)} collective-permute-done((bf16[528,128]{1,0:T(8,128)(2,1)S(1)}, bf16[528,128]{1,0:T(8,128)(2,1)S(1)}, u32[]{:S(2)}, u32[]{:S(2)}) %collective-permute-start.23) | collective-permute-done | bytes 135200 | tf_op jit(solution)/shard_map/ppermute | solution.py:270
  132.4 2.3 %collective-permute-done.24.b = bf16[528,128]{1,0:T(8,128)(2,1)S(1)} collective-permute-done((bf16[528,128]{1,0:T(8,128)(2,1)S(1)}, bf16[528,128]{1,0:T(8,128)(2,1)S(1)}, u32[]{:S(2)}, u32[]{:S(2)}) %collective-permute-start.24) | collective-permute-done | bytes 135200 | tf_op jit(solution)/shard_map/ppermute | solution.py:270
  (55 shorter events, 23.2 us)
Async XLA Ops:
  11.9 3.7 %collective-permute-start = (bf16[16,128,128]{2,1,0:T(8,128)(2,1)S(1)}, bf16[16,128,128]{2,1,0:T(8,128)(2,1)S(1)}, u32[]{:S(2)}, u32[]{:S(2)}) collective-permute-start(bf16[16,128,128]{2,1,0:T(8,128)(2,1)S(1)} %get-tuple-element.26), channel_id=1, source_target_pairs={{0,128},{128,0},{1,129},{129,1},{2,130},{130,2},{3,131},{131,3},{4... | collective-permute-start | bytes 1572872 | tf_op jit(solution)/shard_map/ppermute | solution.py:274
  16.3 7.4 %collective-permute-start.1 = (bf16[4,128,128]{2,1,0:T(8,128)(2,1)S(1)}, bf16[4,128,128]{2,1,0:T(8,128)(2,1)S(1)}, u32[]{:S(2)}, u32[]{:S(2)}) collective-permute-start(bf16[4,128,128]{2,1,0:T(8,128)(2,1)S(1)} %get-tuple-element.28), channel_id=1, source_target_pairs={{0,1},{1,2},{2,3},{3,0},{4,5},{5,6},{6,7},{7,4},{8,9},{9,10},{10,1... | collective-permute-start | bytes 393224 | tf_op jit(solution)/shard_map/ppermute | solution.py:270
  16.8 10.5 %collective-permute-start.2 = (bf16[4,128,128]{2,1,0:T(8,128)(2,1)S(1)}, bf16[4,128,128]{2,1,0:T(8,128)(2,1)S(1)}, u32[]{:S(2)}, u32[]{:S(2)}) collective-permute-start(bf16[4,128,128]{2,1,0:T(8,128)(2,1)S(1)} %get-tuple-element.29), channel_id=1, source_target_pairs={{0,2},{1,3},{2,0},{3,1},{4,6},{5,7},{6,4},{7,5},{8,10},{9,11},{10,... | collective-permute-start | bytes 393224 | tf_op jit(solution)/shard_map/ppermute | solution.py:270
  21.3 6.1 %collective-permute-start.3 = (bf16[4,128,128]{2,1,0:T(8,128)(2,1)S(1)}, bf16[4,128,128]{2,1,0:T(8,128)(2,1)S(1)}, u32[]{:S(2)}, u32[]{:S(2)}) collective-permute-start(bf16[4,128,128]{2,1,0:T(8,128)(2,1)S(1)} %get-tuple-element.30), channel_id=1, source_target_pairs={{0,3},{1,0},{2,1},{3,2},{4,7},{5,4},{6,5},{7,6},{8,11},{9,8},{10,9... | collective-permute-start | bytes 393224 | tf_op jit(solution)/shard_map/ppermute | solution.py:270
  27.8 6.4 %collective-permute-start.6 = (bf16[4,128,128]{2,1,0:T(8,128)(2,1)S(1)}, bf16[4,128,128]{2,1,0:T(8,128)(2,1)S(1)}, u32[]{:S(2)}, u32[]{:S(2)}) collective-permute-start(bf16[4,128,128]{2,1,0:T(8,128)(2,1)S(1)} %first_sum.1.refs_0_), channel_id=1, source_target_pairs={{0,3},{1,0},{2,1},{3,2},{4,7},{5,4},{6,5},{7,6},{8,11},{9,8},{10,9... | collective-permute-start | bytes 393224 | tf_op jit(solution)/shard_map/ppermute | solution.py:270
  30.4 6.6 %collective-permute-start.5 = (bf16[4,128,128]{2,1,0:T(8,128)(2,1)S(1)}, bf16[4,128,128]{2,1,0:T(8,128)(2,1)S(1)}, u32[]{:S(2)}, u32[]{:S(2)}) collective-permute-start(bf16[4,128,128]{2,1,0:T(8,128)(2,1)S(1)} %first_sum.1.refs_0_), channel_id=1, source_target_pairs={{0,2},{1,3},{2,0},{3,1},{4,6},{5,7},{6,4},{7,5},{8,10},{9,11},{10,... | collective-permute-start | bytes 393224 | tf_op jit(solution)/shard_map/ppermute | solution.py:270
  31.1 8.9 %collective-permute-start.4 = (bf16[4,128,128]{2,1,0:T(8,128)(2,1)S(1)}, bf16[4,128,128]{2,1,0:T(8,128)(2,1)S(1)}, u32[]{:S(2)}, u32[]{:S(2)}) collective-permute-start(bf16[4,128,128]{2,1,0:T(8,128)(2,1)S(1)} %first_sum.1.refs_0_), channel_id=1, source_target_pairs={{0,1},{1,2},{2,3},{3,0},{4,5},{5,6},{6,7},{7,4},{8,9},{9,10},{10,1... | collective-permute-start | bytes 393224 | tf_op jit(solution)/shard_map/ppermute | solution.py:270
  31.1 9.5 %collective-permute-start.7 = (bf16[4,128,128]{2,1,0:T(8,128)(2,1)S(1)}, bf16[4,128,128]{2,1,0:T(8,128)(2,1)S(1)}, u32[]{:S(2)}, u32[]{:S(2)}) collective-permute-start(bf16[4,128,128]{2,1,0:T(8,128)(2,1)S(1)} %first_sum.1.refs_0_), channel_id=1, source_target_pairs={{0,128},{128,0},{1,129},{129,1},{2,130},{130,2},{3,131},{131,3},{4... | collective-permute-start | bytes 393224 | tf_op jit(solution)/shard_map/ppermute | solution.py:274
  34.2 6.4 %collective-permute-start.10 = (bf16[4,128,128]{2,1,0:T(8,128)(2,1)S(1)}, bf16[4,128,128]{2,1,0:T(8,128)(2,1)S(1)}, u32[]{:S(2)}, u32[]{:S(2)}) collective-permute-start(bf16[4,128,128]{2,1,0:T(8,128)(2,1)S(1)} %collective-permute-done.6.refs_3_), channel_id=1, source_target_pairs={{0,128},{128,0},{1,129},{129,1},{2,130},{130,2},{3,131},{131,3},{4... | collective-permute-start | bytes 393224 | tf_op jit(solution)/shard_map/ppermute | solution.py:274
  37.0 3.7 %collective-permute-start.9 = (bf16[4,128,128]{2,1,0:T(8,128)(2,1)S(1)}, bf16[4,128,128]{2,1,0:T(8,128)(2,1)S(1)}, u32[]{:S(2)}, u32[]{:S(2)}) collective-permute-start(bf16[4,128,128]{2,1,0:T(8,128)(2,1)S(1)} %collective-permute-done.5.refs_2_), channel_id=1, source_target_pairs={{0,128},{128,0},{1,129},{129,1},{2,130},{130,2},{3,131},{131,3},{4... | collective-permute-start | bytes 393224 | tf_op jit(solution)/shard_map/ppermute | solution.py:274
  46.4 2.7 %collective-permute-start.11 = (bf16[32,128,128]{2,1,0:T(8,128)(2,1)S(1)}, bf16[32,128,128]{2,1,0:T(8,128)(2,1)S(1)}, u32[]{:S(2)}, u32[]{:S(2)}) collective-permute-start(bf16[32,128,128]{2,1,0:T(8,128)(2,1)S(1)} %get-tuple-element.32), channel_id=1, source_target_pairs={{0,128},{128,0},{1,129},{129,1},{2,130},{130,2},{3,131},{131,3},{4... | collective-permute-start | bytes 3145736 | tf_op jit(solution)/shard_map/ppermute | solution.py:274
  50.1 14.7 %collective-permute-start.12 = (bf16[8,128,128]{2,1,0:T(8,128)(2,1)S(1)}, bf16[8,128,128]{2,1,0:T(8,128)(2,1)S(1)}, u32[]{:S(2)}, u32[]{:S(2)}) collective-permute-start(bf16[8,128,128]{2,1,0:T(8,128)(2,1)S(1)} %get-tuple-element.34), channel_id=1, source_target_pairs={{0,32},{32,64},{64,96},{96,0},{1,33},{33,65},{65,97},{97,1},{2,34}... | collective-permute-start | bytes 786440 | tf_op jit(solution)/shard_map/ppermute | solution.py:270
  50.4 14.3 %collective-permute-start.13 = (bf16[8,128,128]{2,1,0:T(8,128)(2,1)S(1)}, bf16[8,128,128]{2,1,0:T(8,128)(2,1)S(1)}, u32[]{:S(2)}, u32[]{:S(2)}) collective-permute-start(bf16[8,128,128]{2,1,0:T(8,128)(2,1)S(1)} %get-tuple-element.35), channel_id=1, source_target_pairs={{0,64},{32,96},{64,0},{96,32},{1,65},{33,97},{65,1},{97,33},{2,66}... | collective-permute-start | bytes 786440 | tf_op jit(solution)/shard_map/ppermute | solution.py:270
  52.1 13.0 %collective-permute-start.14 = (bf16[8,128,128]{2,1,0:T(8,128)(2,1)S(1)}, bf16[8,128,128]{2,1,0:T(8,128)(2,1)S(1)}, u32[]{:S(2)}, u32[]{:S(2)}) collective-permute-start(bf16[8,128,128]{2,1,0:T(8,128)(2,1)S(1)} %get-tuple-element.36), channel_id=1, source_target_pairs={{0,96},{32,0},{64,32},{96,64},{1,97},{33,1},{65,33},{97,65},{2,98}... | collective-permute-start | bytes 786440 | tf_op jit(solution)/shard_map/ppermute | solution.py:270
  96.7 9.6 %collective-permute-start.17 = (bf16[8,128,128]{2,1,0:T(8,128)(2,1)S(1)}, bf16[8,128,128]{2,1,0:T(8,128)(2,1)S(1)}, u32[]{:S(2)}, u32[]{:S(2)}) collective-permute-start(bf16[8,128,128]{2,1,0:T(8,128)(2,1)S(1)} %all_to_all.11.refs_0_), channel_id=1, source_target_pairs={{0,96},{32,0},{64,32},{96,64},{1,97},{33,1},{65,33},{97,65},{2,98}... | collective-permute-start | bytes 786440 | tf_op jit(solution)/shard_map/ppermute | solution.py:270
  100.1 12.1 %collective-permute-start.16 = (bf16[8,128,128]{2,1,0:T(8,128)(2,1)S(1)}, bf16[8,128,128]{2,1,0:T(8,128)(2,1)S(1)}, u32[]{:S(2)}, u32[]{:S(2)}) collective-permute-start(bf16[8,128,128]{2,1,0:T(8,128)(2,1)S(1)} %all_to_all.11.refs_0_), channel_id=1, source_target_pairs={{0,64},{32,96},{64,0},{96,32},{1,65},{33,97},{65,1},{97,33},{2,66}... | collective-permute-start | bytes 786440 | tf_op jit(solution)/shard_map/ppermute | solution.py:270
  100.7 13.1 %collective-permute-start.15 = (bf16[8,128,128]{2,1,0:T(8,128)(2,1)S(1)}, bf16[8,128,128]{2,1,0:T(8,128)(2,1)S(1)}, u32[]{:S(2)}, u32[]{:S(2)}) collective-permute-start(bf16[8,128,128]{2,1,0:T(8,128)(2,1)S(1)} %all_to_all.11.refs_0_), channel_id=1, source_target_pairs={{0,32},{32,64},{64,96},{96,0},{1,33},{33,65},{65,97},{97,1},{2,34}... | collective-permute-start | bytes 786440 | tf_op jit(solution)/shard_map/ppermute | solution.py:270
  100.7 15.3 %collective-permute-start.18 = (bf16[8,128,128]{2,1,0:T(8,128)(2,1)S(1)}, bf16[8,128,128]{2,1,0:T(8,128)(2,1)S(1)}, u32[]{:S(2)}, u32[]{:S(2)}) collective-permute-start(bf16[8,128,128]{2,1,0:T(8,128)(2,1)S(1)} %all_to_all.11.refs_0_), channel_id=1, source_target_pairs={{0,128},{128,0},{1,129},{129,1},{2,130},{130,2},{3,131},{131,3},{4... | collective-permute-start | bytes 786440 | tf_op jit(solution)/shard_map/ppermute | solution.py:274
  106.3 9.7 %collective-permute-start.21 = (bf16[8,128,128]{2,1,0:T(8,128)(2,1)S(1)}, bf16[8,128,128]{2,1,0:T(8,128)(2,1)S(1)}, u32[]{:S(2)}, u32[]{:S(2)}) collective-permute-start(bf16[8,128,128]{2,1,0:T(8,128)(2,1)S(1)} %collective-permute-done.17.refs_3_), channel_id=1, source_target_pairs={{0,128},{128,0},{1,129},{129,1},{2,130},{130,2},{3,131},{131,3},{4... | collective-permute-start | bytes 786440 | tf_op jit(solution)/shard_map/ppermute | solution.py:274
  112.3 3.7 %collective-permute-start.20 = (bf16[8,128,128]{2,1,0:T(8,128)(2,1)S(1)}, bf16[8,128,128]{2,1,0:T(8,128)(2,1)S(1)}, u32[]{:S(2)}, u32[]{:S(2)}) collective-permute-start(bf16[8,128,128]{2,1,0:T(8,128)(2,1)S(1)} %collective-permute-done.16.refs_2_), channel_id=1, source_target_pairs={{0,128},{128,0},{1,129},{129,1},{2,130},{130,2},{3,131},{131,3},{4... | collective-permute-start | bytes 786440 | tf_op jit(solution)/shard_map/ppermute | solution.py:274
  113.8 3.3 %collective-permute-start.19 = (bf16[8,128,128]{2,1,0:T(8,128)(2,1)S(1)}, bf16[8,128,128]{2,1,0:T(8,128)(2,1)S(1)}, u32[]{:S(2)}, u32[]{:S(2)}) collective-permute-start(bf16[8,128,128]{2,1,0:T(8,128)(2,1)S(1)} %collective-permute-done.15.refs_1_), channel_id=1, source_target_pairs={{0,128},{128,0},{1,129},{129,1},{2,130},{130,2},{3,131},{131,3},{4... | collective-permute-start | bytes 786440 | tf_op jit(solution)/shard_map/ppermute | solution.py:274
  125.7 6.7 %collective-permute-start.23 = (bf16[528,128]{1,0:T(8,128)(2,1)S(1)}, bf16[528,128]{1,0:T(8,128)(2,1)S(1)}, u32[]{:S(2)}, u32[]{:S(2)}) collective-permute-start(bf16[528,128]{1,0:T(8,128)(2,1)S(1)} %get-tuple-element.43), channel_id=1, source_target_pairs={{0,1},{1,2},{2,3},{3,0},{4,5},{5,6},{6,7},{7,4},{8,9},{9,10},{10,1... | collective-permute-start | bytes 405512 | tf_op jit(solution)/shard_map/ppermute | solution.py:270
  125.8 8.8 %collective-permute-start.24 = (bf16[528,128]{1,0:T(8,128)(2,1)S(1)}, bf16[528,128]{1,0:T(8,128)(2,1)S(1)}, u32[]{:S(2)}, u32[]{:S(2)}) collective-permute-start(bf16[528,128]{1,0:T(8,128)(2,1)S(1)} %get-tuple-element.44), channel_id=1, source_target_pairs={{0,2},{1,3},{2,0},{3,1},{4,6},{5,7},{6,4},{7,5},{8,10},{9,11},{10,... | collective-permute-start | bytes 405512 | tf_op jit(solution)/shard_map/ppermute | solution.py:270
  128.4 6.9 %collective-permute-start.25 = (bf16[528,128]{1,0:T(8,128)(2,1)S(1)}, bf16[528,128]{1,0:T(8,128)(2,1)S(1)}, u32[]{:S(2)}, u32[]{:S(2)}) collective-permute-start(bf16[528,128]{1,0:T(8,128)(2,1)S(1)} %get-tuple-element.45), channel_id=1, source_target_pairs={{0,3},{1,0},{2,1},{3,2},{4,7},{5,4},{6,5},{7,6},{8,11},{9,8},{10,9... | collective-permute-start | bytes 405512 | tf_op jit(solution)/shard_map/ppermute | solution.py:270
  (9 other events, 103.3 us)

commit v2 on v1

v2 whole, which is shorter than its diff:
```python
import jax
import jax.numpy as jnp
from jax import lax
from jax.experimental import pallas as pl
from jax.experimental.pallas import tpu as pltpu
from jax.sharding import Mesh
from jax.sharding import PartitionSpec as P

TILE = 128
RANK = 128
CTILES = 32
DTILES = 64
NX = 4
NZ = 8
NCOL = 4
NDST = 32768
BLOCK = 64
UNROLL = 32
EPS = 1e-06

F32 = jnp.float32
BF16 = jnp.bfloat16
CORE, XPOS, COL = 0, 1, 2

SMEM = pl.BlockSpec(memory_space=pltpu.SMEM)
VMEM = pl.BlockSpec(memory_space=pltpu.VMEM)
HBM = pl.BlockSpec(memory_space=pltpu.HBM)
PARAMS = pltpu.CompilerParams(vmem_limit_bytes=40 * 2**20)


def tiles_of(n, dtype):
    return jax.ShapeDtypeStruct((n, TILE, RANK), dtype)


def each(n, body):
    def step(i, carry):
        body(i)
        return carry

    lax.fori_loop(0, n, step, 0)


def accumulate(first, size, dst, src, count, tiles, panel, acc, dump, tile_left):
    live = count[0]
    left = jnp.clip(live - first, 0, size)

    def group(g, carry):
        for j in range(UNROLL):
            t = first + g * UNROLL + j
            d = jnp.where(t < live, dst[t], dump)
            tile, block = tiles[t], panel[src[t]]
            a, b = (tile, block) if tile_left else (block, tile)
            acc[d] += jnp.dot(a, b, preferred_element_type=F32)
        return carry

    lax.fori_loop(0, (left + UNROLL - 1) // UNROLL, group, 0)


def split(ids, acc, keep, send, half):
    core = ids[CORE]

    def one(i):
        keep[i] = acc[core * half + i]
        send[i] = acc[(1 - core) * half + i].astype(BF16)

    each(half, one)


def zero(acc):
    def one(i):
        acc[i] = jnp.zeros((TILE, RANK), F32)

    each(acc.shape[0], one)


def place(ids, parts, panel, axis, n, per):
    core, me = ids[CORE], ids[axis]
    for side in range(2):
        base = jnp.where(side == 0, core, 1 - core) * (n * per)
        for k in range(n):
            at = base + lax.rem(me + n - k, n) * per
            part = parts[side * n + k]

            def one(i):
                panel[at + i] = part[i]

            each(per, one)


def first_kernel(dst_hbm, src_hbm, count, ids, tiles_hbm, panel_hbm, keep, send, tiles, dst, src, panel, acc, sems):
    n_blocks = tiles.shape[0] // BLOCK
    lists = [
        pltpu.make_async_copy(dst_hbm, dst, sems.at[0]),
        pltpu.make_async_copy(src_hbm, src, sems.at[1]),
        pltpu.make_async_copy(panel_hbm, panel, sems.at[2]),
    ]
    blocks = [
        pltpu.make_async_copy(
            tiles_hbm.at[pl.ds(i * BLOCK, BLOCK)], tiles.at[pl.ds(i * BLOCK, BLOCK)], sems.at[3 + i]
        )
        for i in range(n_blocks)
    ]
    for copy in lists + blocks:
        copy.start()
    zero(acc)
    for copy in lists:
        copy.wait()
    for i in range(n_blocks):
        blocks[i].wait()
        accumulate(i * BLOCK, BLOCK, dst, src, count, tiles, panel, acc, CTILES, True)
    split(ids, acc, keep, send, CTILES // 2)


def in_hbm(value):
    return pltpu.with_memory_space_constraint(value, pltpu.HBM)


def first_pass(rows, cols, count, ids, tiles, start):
    return pl.pallas_call(
        first_kernel,
        in_specs=[HBM, HBM, SMEM, SMEM, HBM, HBM],
        out_specs=[VMEM] * 3,
        out_shape=[tiles_of(CTILES // 2, F32), tiles_of(CTILES // 2, BF16), tiles_of(tiles.shape[0], BF16)],
        scratch_shapes=[
            pltpu.SMEM(rows.shape, jnp.int32),
            pltpu.SMEM(cols.shape, jnp.int32),
            pltpu.VMEM(start.shape, BF16),
            pltpu.VMEM((CTILES + 1, TILE, RANK), F32),
            pltpu.SemaphoreType.DMA((3 + tiles.shape[0] // BLOCK,)),
        ],
        compiler_params=pltpu.CompilerParams(vmem_limit_bytes=40 * 2**20),
        name="first_pass",
    )(*(in_hbm(v) for v in (rows, cols)), count, ids, *(in_hbm(v) for v in (tiles, start)))


def back_kernel(dst, src, count, ids, tiles, *refs):
    parts, (keep, send, panel, acc) = refs[: 2 * NCOL], refs[2 * NCOL :]
    zero(acc)
    place(ids, parts, panel, COL, NCOL, CTILES // 2 // NCOL)
    accumulate(0, tiles.shape[0], dst, src, count, tiles, panel, acc, DTILES, False)
    split(ids, acc, keep, send, DTILES // 2)


def last_kernel(dst, src, count, ids, tiles, *refs):
    parts, (keep, send, squares, panel, acc) = refs[: 2 * NX], refs[2 * NX :]
    zero(acc)
    place(ids, parts, panel, XPOS, NX, NZ)
    accumulate(0, tiles.shape[0], dst, src, count, tiles, panel, acc, CTILES, True)
    split(ids, acc, keep, send, CTILES // 2)

    def one(i, total):
        block = panel[i].astype(F32)
        return total + jnp.sum((block * block).reshape(TILE // 8, 8, RANK), axis=0)

    squares[...] = lax.fori_loop(0, DTILES, one, jnp.zeros((8, RANK), F32))


def tile_pass(kernel, dst, src, count, ids, tiles, parts, n_acc, panel_tiles, extra, name):
    half = n_acc // 2
    return pl.pallas_call(
        kernel,
        in_specs=[SMEM] * 4 + [VMEM] * (1 + len(parts)),
        out_specs=[VMEM] * (2 + len(extra)),
        out_shape=[tiles_of(half, F32), tiles_of(half, BF16)] + extra,
        scratch_shapes=[
            pltpu.VMEM((panel_tiles, TILE, RANK), BF16),
            pltpu.VMEM((n_acc + 1, TILE, RANK), F32),
        ],
        compiler_params=PARAMS,
        name=name,
    )(dst, src, count, ids, tiles, *parts)


def first_pair_kernel(ids, keep, got, own, *sends):
    me = ids[COL]
    per = own.shape[0]
    for k in range(NCOL):
        base = lax.rem(me + k, NCOL) * per

        def one(i):
            total = keep[base + i] + got[base + i].astype(F32)
            if k == 0:
                own[i] = total
            else:
                sends[k - 1][i] = total.astype(BF16)

        each(per, one)


def back_pair_kernel(keep, got, out):
    def one(i):
        out[i] = (keep[i] + got[i].astype(F32)).astype(BF16)

    each(out.shape[0], one)


def caller_kernel(own, a, b, c, out):
    def one(i):
        total = own[i] + a[i].astype(F32) + b[i].astype(F32) + c[i].astype(F32)
        out[i] = total.astype(BF16).astype(F32).T.astype(BF16)

    each(own.shape[0], one)


def share_kernel(got, share, copies):
    total = got[0].astype(F32)
    for k in range(1, NX * NZ):
        total += got[k].astype(F32)
    total = total.T
    share[...] = total
    for k in range(NZ):
        copies[k] = total.astype(BF16)


def last_pair_kernel(ids, keep, got, squares, own, *sends):
    me = ids[COL]
    per = CTILES // 2 // NCOL
    total = jnp.sum(squares[...], axis=0, keepdims=True)
    high = total.astype(BF16).astype(F32)
    middle = (total - high).astype(BF16).astype(F32)
    low = total - high - middle
    row = lax.broadcasted_iota(jnp.int32, (16, RANK), 0)
    coded = jnp.where(row == 0, high, jnp.where(row == 1, middle, jnp.where(row == 2, low, 0.0)))
    for k in range(NCOL):
        base = lax.rem(me + k, NCOL) * per
        if k:
            sends[k - 1][pl.ds(per * TILE, 16), :] = coded.astype(BF16)
        for i in range(per):
            part = keep[base + i] + got[base + i].astype(F32)
            if k == 0:
                own[i] = part
            else:
                sends[k - 1][pl.ds(i * TILE, TILE), :] = part.astype(BF16)


def final_kernel(own, squares, share, a, b, c, caller, dest):
    per = CTILES // 2 // NCOL
    total = jnp.sum(squares[...], axis=0, keepdims=True)
    for got in (a, b, c):
        total += jnp.sum(got[pl.ds(per * TILE, 16), :].astype(F32), axis=0, keepdims=True)
    scale = lax.rsqrt(total / NDST + EPS)
    dest[...] = (share[...] * scale).astype(BF16)
    for i in range(per):
        at = pl.ds(i * TILE, TILE)
        part = own[i] + a[at, :].astype(F32) + b[at, :].astype(F32) + c[at, :].astype(F32)
        caller[at, :] = (part * scale).astype(BF16)


def shifted(value, axis, k, n):
    return lax.ppermute(value, axis, [(i, (i + k) % n) for i in range(n)])


def swap(value):
    return lax.ppermute(value, "layer", [(0, 1), (1, 0)])


def exchange(values, axis, n):
    return [shifted(v, axis, k + 1, n) for k, v in enumerate(values)]


def gather(value, axis, n):
    mine = [value] + [shifted(value, axis, k, n) for k in range(1, n)]
    return mine + [swap(v) for v in mine]


def on_device(tile_values, tile_rows, tile_cols, tile_count, start_panel):
    tiles = tile_values[0, 0, 0]
    rows = tile_rows[0, 0, 0]
    cols = tile_cols[0, 0, 0]
    count = tile_count[0, 0]
    ids = jnp.stack([lax.axis_index(a) for a in ("layer", "x", "col")]).astype(jnp.int32)
    start = start_panel.reshape(DTILES, TILE, RANK)
    quarter = CTILES // 2 // NCOL

    keep, send, tiles = first_pass(rows, cols, count, ids, tiles, start)
    own, *sends = pl.pallas_call(
        first_pair_kernel,
        in_specs=[SMEM, VMEM, VMEM],
        out_specs=[VMEM] * NCOL,
        out_shape=[tiles_of(quarter, F32)] + [tiles_of(quarter, BF16)] * (NCOL - 1),
        compiler_params=PARAMS,
        name="first_pair",
    )(ids, keep, swap(send))
    part = pl.pallas_call(
        caller_kernel,
        in_specs=[VMEM] * NCOL,
        out_specs=VMEM,
        out_shape=tiles_of(quarter, BF16),
        compiler_params=PARAMS,
        name="first_sum",
    )(own, *exchange(sends, "col", NCOL))
    parts = gather(part, "col", NCOL)

    keep, send = tile_pass(back_kernel, cols, rows, count, ids, tiles, parts, DTILES, CTILES, [], "back_pass")
    part = pl.pallas_call(
        back_pair_kernel,
        in_specs=[VMEM, VMEM],
        out_specs=VMEM,
        out_shape=tiles_of(DTILES // 2, BF16),
        compiler_params=PARAMS,
        name="back_pair",
    )(keep, swap(send))
    got = lax.all_to_all(part, ("x", "z"), split_axis=0, concat_axis=0, tiled=True)
    share, copies = pl.pallas_call(
        share_kernel,
        in_specs=[VMEM],
        out_specs=[VMEM, VMEM],
        out_shape=[jax.ShapeDtypeStruct((TILE, RANK), F32), tiles_of(NZ, BF16)],
        compiler_params=PARAMS,
        name="share_sum",
    )(got)
    part = lax.all_to_all(copies, "z", split_axis=0, concat_axis=0, tiled=True)
    parts = gather(part, "x", NX)

    keep, send, squares = tile_pass(
        last_kernel, rows, cols, count, ids, tiles, parts, CTILES, DTILES,
        [jax.ShapeDtypeStruct((8, RANK), F32)], "last_pass",
    )
    chunk = jax.ShapeDtypeStruct((quarter * TILE + 16, RANK), BF16)
    own, *sends = pl.pallas_call(
        last_pair_kernel,
        in_specs=[SMEM, VMEM, VMEM, VMEM],
        out_specs=[VMEM] * NCOL,
        out_shape=[tiles_of(quarter, F32)] + [chunk] * (NCOL - 1),
        compiler_params=PARAMS,
        name="last_pair",
    )(ids, keep, swap(send), squares)
    got = exchange(sends, "col", NCOL)
    caller, dest = pl.pallas_call(
        final_kernel,
        in_specs=[VMEM] * 6,
        out_specs=[VMEM, VMEM],
        out_shape=[
            jax.ShapeDtypeStruct((quarter * TILE, RANK), BF16),
            jax.ShapeDtypeStruct((TILE, RANK), BF16),
        ],
        compiler_params=PARAMS,
        name="final",
    )(own, squares, share, *got)
    return caller[None], dest[None]


def solution(mesh):
    fine = Mesh(mesh.devices.reshape(2, NX, NZ, NCOL), ("layer", "x", "z", "col"))
    row = ("x", "z")
    placed = (
        P("layer", row, "col", None, None, None),
        P("layer", row, "col", None),
        P("layer", row, "col", None),
        P("layer", row, "col"),
        P("col", None),
    )
    return jax.shard_map(
        on_device,
        mesh=fine,
        in_specs=placed,
        out_specs=(P(row, ("layer", "col"), None), P("col", ("layer", "x", "z"), None)),
        check_vma=False,
    )
```

time: 137 us -> 133 us (0.971)
  blocking collectives: 31.4 us -> 52.3 us
  waiting for transfers between devices: 36.7 us -> 27.1 us
  starting transfers between devices: 41.4 us -> 34.8 us
  local copies, waits for them, and re-layouts: 6.35 us -> 0.01 us
  Pallas kernels: 18.6 us -> 16.4 us
    all_to_all x1, blocking collectives: 19.5 us -> 37.4 us  [on_device(): lax.all_to_all(part, ('x', 'z'), split_axis=0, concat_axis=0, tiled=True)]
    ppermute x15 -> x12, waiting for transfers between devices: 28.5 us -> 19.6 us  [shifted(): return lax.ppermute(value, axis, [(i, (i + k) % n) for i in range(n)])]
    unnamed x14 -> x4, local copies, waits for them, and re-layouts: 6.35 us -> 0.01 us
    ppermute x15 -> x12, starting transfers between devices: 19.1 us -> 14 us  [shifted(): return lax.ppermute(value, axis, [(i, (i + k) % n) for i in range(n)])]
    all_to_all x1, blocking collectives: 11.9 us -> 14.9 us  [on_device(): part = lax.all_to_all(copies, 'z', split_axis=0, concat_axis=0, tiled=True)]
    pallas_call x7 -> x6, Pallas kernels: 17.1 us -> 14.8 us  [the longest x2 8.23 us: tile_pass(): pl.pallas_call(kernel, in_specs=[SMEM] * 4 + [VMEM] * (1 + len(parts)), o...]
    ppermute x11, starting transfers between devices: 22.2 us -> 20.8 us  [swap(): return lax.ppermute(value, 'layer', [(0, 1), (1, 0)])]
  transfers between devices with their start and end apart: 26 -> 23, of which waited for: 16 -> 15; matrix products, arithmetic and copies ran while one was open for 0% -> 0% of each run, Pallas kernels for 0% -> 0%
where the time goes in v2:
time: 133 us; the launch traced here: 132 us
  blocking collectives  52.3 us (39%)
  starting transfers between devices  34.8 us (26%)
  waiting for transfers between devices  27.1 us (20%)
  Pallas kernels  16.4 us (12%)
  between operations  1.4 us (1%)
    all_to_all x1, blocking collectives, on_device(): lax.all_to_all(part, ('x', 'z'), split_axis=0, concat_axis=0, tiled=True)  37.4 us
    ppermute x11, starting transfers between devices, swap(): return lax.ppermute(value, 'layer', [(0, 1), (1, 0)])  20.8 us
    ppermute x12, waiting for transfers between devices, shifted(): return lax.ppermute(value, axis, [(i, (i + k) % n) for i in range(n)])  19.6 us
    all_to_all x1, blocking collectives, on_device(): part = lax.all_to_all(copies, 'z', split_axis=0, concat_axis=0, tiled=True)  14.9 us
    ppermute x12, starting transfers between devices, shifted(): return lax.ppermute(value, axis, [(i, (i + k) % n) for i in range(n)])  14 us
    pallas_call x2, Pallas kernels, tile_pass(): pl.pallas_call(kernel, in_specs=[SMEM] * 4 + [VMEM] * (1 + len(parts)), o...  8.23 us
    ppermute x11, waiting for transfers between devices, swap(): return lax.ppermute(value, 'layer', [(0, 1), (1, 0)])  7.51 us
    pallas_call x1, Pallas kernels, first_pass(): pl.pallas_call(first_kernel, in_specs=[HBM, HBM, SMEM, SMEM, HBM, HBM], o...  5.08 us
  transfers between devices with their start and end apart: 23, of which 15 were waited for; matrix products, arithmetic and copies ran while one was open for 0% of the time, Pallas kernels for 0%

profile of v2, /device:TPU:1, one launch (start us, length us, event | category | flops | bytes accessed | tf_op | source)
XLA Modules:
  0.0 132.1 jit_solution(17680297495425519060)
XLA Ops:
  1.4 5.1 %first_pass.1 = (f32[16,128,128]{2,1,0:T(8,128)S(1)}, bf16[16,128,128]{2,1,0:T(8,128)(2,1)S(1)}, bf16[256,128,128]{2,1,0:T(8,128)(2,1)S(1)}) custom-call(s32[256]{0:T(256)} %bitcast.13, s32[256]{0:T(256)} %bitcast.16, s32[1]{0:T(128)} %bitcast.10.count, s32[3]{0:T(128)S(1)} %pad_add_fusion.ids, bf16[256,128,128]{2,1,0:T(8,128)(2,1)} %bitcast.19, ...), custom_call_target="tpu_custom_call" | custom-call | tf_op jit(solution)/shard_map/first_pass/pallas_call | solution.py:119
  6.5 3.3 %collective-permute-start = (bf16[16,128,128]{2,1,0:T(8,128)(2,1)S(1)}, bf16[16,128,128]{2,1,0:T(8,128)(2,1)S(1)}, u32[]{:S(2)}, u32[]{:S(2)}) collective-permute-start(bf16[16,128,128]{2,1,0:T(8,128)(2,1)S(1)} %get-tuple-element.24), channel_id=1, source_target_pairs={{0,128},{128,0},{1,129},{129,1},{2,130},{130,2},{3,131},{131,3},{4... | collective-permute-start | bytes 1572872 | tf_op jit(solution)/shard_map/ppermute | solution.py:254
  9.8 1.5 %collective-permute-done.got = bf16[16,128,128]{2,1,0:T(8,128)(2,1)S(1)} collective-permute-done((bf16[16,128,128]{2,1,0:T(8,128)(2,1)S(1)}, bf16[16,128,128]{2,1,0:T(8,128)(2,1)S(1)}, u32[]{:S(2)}, u32[]{:S(2)}) %collective-permute-start) | collective-permute-done | bytes 524320 | tf_op jit(solution)/shard_map/ppermute | solution.py:254
  12.2 2.2 %collective-permute-start.2 = (bf16[4,128,128]{2,1,0:T(8,128)(2,1)S(1)}, bf16[4,128,128]{2,1,0:T(8,128)(2,1)S(1)}, u32[]{:S(2)}, u32[]{:S(2)}) collective-permute-start(bf16[4,128,128]{2,1,0:T(8,128)(2,1)S(1)} %get-tuple-element.27), channel_id=1, source_target_pairs={{0,2},{1,3},{2,0},{3,1},{4,6},{5,7},{6,4},{7,5},{8,10},{9,11},{10,... | collective-permute-start | bytes 393224 | tf_op jit(solution)/shard_map/ppermute | solution.py:250
  15.2 3.4 %collective-permute-done.1.a = bf16[4,128,128]{2,1,0:T(8,128)(2,1)S(1)} collective-permute-done((bf16[4,128,128]{2,1,0:T(8,128)(2,1)S(1)}, bf16[4,128,128]{2,1,0:T(8,128)(2,1)S(1)}, u32[]{:S(2)}, u32[]{:S(2)}) %collective-permute-start.1) | collective-permute-done | bytes 131104 | tf_op jit(solution)/shard_map/ppermute | solution.py:250
  18.6 1.9 %collective-permute-done.2.b = bf16[4,128,128]{2,1,0:T(8,128)(2,1)S(1)} collective-permute-done((bf16[4,128,128]{2,1,0:T(8,128)(2,1)S(1)}, bf16[4,128,128]{2,1,0:T(8,128)(2,1)S(1)}, u32[]{:S(2)}, u32[]{:S(2)}) %collective-permute-start.2) | collective-permute-done | bytes 131104 | tf_op jit(solution)/shard_map/ppermute | solution.py:250
  21.6 3.5 %collective-permute-start.6 = (bf16[4,128,128]{2,1,0:T(8,128)(2,1)S(1)}, bf16[4,128,128]{2,1,0:T(8,128)(2,1)S(1)}, u32[]{:S(2)}, u32[]{:S(2)}) collective-permute-start(bf16[4,128,128]{2,1,0:T(8,128)(2,1)S(1)} %first_sum.1.refs_0_), channel_id=1, source_target_pairs={{0,3},{1,0},{2,1},{3,2},{4,7},{5,4},{6,5},{7,6},{8,11},{9,8},{10,9... | collective-permute-start | bytes 393224 | tf_op jit(solution)/shard_map/ppermute | solution.py:250
  26.8 3.6 %collective-permute-done.6.refs_3_ = bf16[4,128,128]{2,1,0:T(8,128)(2,1)S(1)} collective-permute-done((bf16[4,128,128]{2,1,0:T(8,128)(2,1)S(1)}, bf16[4,128,128]{2,1,0:T(8,128)(2,1)S(1)}, u32[]{:S(2)}, u32[]{:S(2)}) %collective-permute-start.6) | collective-permute-done | bytes 131104 | tf_op jit(solution)/shard_map/ppermute | solution.py:250
  30.4 1.2 collective-permute-start.10
  31.6 2.2 %collective-permute-start.9 = (bf16[4,128,128]{2,1,0:T(8,128)(2,1)S(1)}, bf16[4,128,128]{2,1,0:T(8,128)(2,1)S(1)}, u32[]{:S(2)}, u32[]{:S(2)}) collective-permute-start(bf16[4,128,128]{2,1,0:T(8,128)(2,1)S(1)} %collective-permute-done.5.refs_2_), channel_id=1, source_target_pairs={{0,128},{128,0},{1,129},{129,1},{2,130},{130,2},{3,131},{131,3},{4... | collective-permute-start | bytes 393224 | tf_op jit(solution)/shard_map/ppermute | solution.py:254
  36.0 3.5 %back_pass.1 = (f32[32,128,128]{2,1,0:T(8,128)S(1)}, bf16[32,128,128]{2,1,0:T(8,128)(2,1)S(1)}) custom-call(s32[256]{0:T(256)S(1)} %bitcast.17, s32[256]{0:T(256)S(1)} %bitcast.14, s32[1]{0:T(128)} %bitcast.11.count, s32[3]{0:T(128)S(1)} %pad_add_fusion.ids, bf16[256,128,128]{2,1,0:T(8,128)(2,1)S(1)} %get-tuple-element.22.tiles, ...), custom_call_target="tpu_custom_call" | custom-call | tf_op jit(solution)/shard_map/back_pass/pallas_call | solution.py:160
  40.0 2.3 %collective-permute-done.11.got = bf16[32,128,128]{2,1,0:T(8,128)(2,1)S(1)} collective-permute-done((bf16[32,128,128]{2,1,0:T(8,128)(2,1)S(1)}, bf16[32,128,128]{2,1,0:T(8,128)(2,1)S(1)}, u32[]{:S(2)}, u32[]{:S(2)}) %collective-permute-start.11) | collective-permute-done | bytes 1048608 | tf_op jit(solution)/shard_map/ppermute | solution.py:254
  42.6 37.4 %all_to_all.10.got = bf16[32,128,128]{2,1,0:T(8,128)(2,1)S(1)} all-to-all(bf16[32,128,128]{2,1,0:T(8,128)(2,1)S(1)} %back_pair.1), channel_id=1, replica_groups=mesh['layer'=2,'x'=4,'z'=8,'col'=4] {'x','z'}, dimensions={0} | all-to-all | bytes 2097152 | tf_op jit(solution)/shard_map/all_to_all | solution.py:303
  80.2 14.9 %all_to_all.11.refs_0_ = bf16[8,128,128]{2,1,0:T(8,128)(2,1)S(1)} all-to-all(bf16[8,128,128]{2,1,0:T(8,128)(2,1)S(1)} %get-tuple-element.31), channel_id=1, replica_groups=mesh['layer'=2,'x'=4,'z'=8,'col'=4] {'z'}, dimensions={0} | all-to-all | bytes 524288 | tf_op jit(solution)/shard_map/all_to_all | solution.py:312
  95.1 2.7 %collective-permute-start.14 = (bf16[8,128,128]{2,1,0:T(8,128)(2,1)S(1)}, bf16[8,128,128]{2,1,0:T(8,128)(2,1)S(1)}, u32[]{:S(2)}, u32[]{:S(2)}) collective-permute-start(bf16[8,128,128]{2,1,0:T(8,128)(2,1)S(1)} %all_to_all.11.refs_0_), channel_id=1, source_target_pairs={{0,96},{32,0},{64,32},{96,64},{1,97},{33,1},{65,33},{97,65},{2,98}... | collective-permute-start | bytes 786440 | tf_op jit(solution)/shard_map/ppermute | solution.py:250
  98.8 3.6 %collective-permute-start.15 = (bf16[8,128,128]{2,1,0:T(8,128)(2,1)S(1)}, bf16[8,128,128]{2,1,0:T(8,128)(2,1)S(1)}, u32[]{:S(2)}, u32[]{:S(2)}) collective-permute-start(bf16[8,128,128]{2,1,0:T(8,128)(2,1)S(1)} %all_to_all.11.refs_0_), channel_id=1, source_target_pairs={{0,128},{128,0},{1,129},{129,1},{2,130},{130,2},{3,131},{131,3},{4... | collective-permute-start | bytes 786440 | tf_op jit(solution)/shard_map/ppermute | solution.py:254
  102.4 2.4 %collective-permute-done.14.refs_3_ = bf16[8,128,128]{2,1,0:T(8,128)(2,1)S(1)} collective-permute-done((bf16[8,128,128]{2,1,0:T(8,128)(2,1)S(1)}, bf16[8,128,128]{2,1,0:T(8,128)(2,1)S(1)}, u32[]{:S(2)}, u32[]{:S(2)}) %collective-permute-start.14) | collective-permute-done | bytes 262176 | tf_op jit(solution)/shard_map/ppermute | solution.py:250
  104.8 5.1 %collective-permute-start.18 = (bf16[8,128,128]{2,1,0:T(8,128)(2,1)S(1)}, bf16[8,128,128]{2,1,0:T(8,128)(2,1)S(1)}, u32[]{:S(2)}, u32[]{:S(2)}) collective-permute-start(bf16[8,128,128]{2,1,0:T(8,128)(2,1)S(1)} %collective-permute-done.14.refs_3_), channel_id=1, source_target_pairs={{0,128},{128,0},{1,129},{129,1},{2,130},{130,2},{3,131},{131,3},{4... | collective-permute-start | bytes 786440 | tf_op jit(solution)/shard_map/ppermute | solution.py:254
  111.9 1.6 %collective-permute-start.16 = (bf16[8,128,128]{2,1,0:T(8,128)(2,1)S(1)}, bf16[8,128,128]{2,1,0:T(8,128)(2,1)S(1)}, u32[]{:S(2)}, u32[]{:S(2)}) collective-permute-start(bf16[8,128,128]{2,1,0:T(8,128)(2,1)S(1)} %collective-permute-done.12.refs_1_), channel_id=1, source_target_pairs={{0,128},{128,0},{1,129},{129,1},{2,130},{130,2},{3,131},{131,3},{4... | collective-permute-start | bytes 786440 | tf_op jit(solution)/shard_map/ppermute | solution.py:254
  114.7 4.7 %last_pass.1 = (f32[16,128,128]{2,1,0:T(8,128)S(1)}, bf16[16,128,128]{2,1,0:T(8,128)(2,1)S(1)}, f32[8,128]{1,0:T(8,128)S(1)}) custom-call(s32[256]{0:T(256)S(1)} %bitcast.15, s32[256]{0:T(256)S(1)} %bitcast.18, s32[1]{0:T(128)} %bitcast.12.count, s32[3]{0:T(128)S(1)} %pad_add_fusion.ids, bf16[256,128,128]{2,1,0:T(8,128)(2,1)S(1)} %get-tuple-element.22.tiles, ...), custom_call_target="tpu_custom_call" | custom-call | tf_op jit(solution)/shard_map/last_pass/pallas_call | solution.py:160
  119.8 1.5 %collective-permute-done.19.got = bf16[16,128,128]{2,1,0:T(8,128)(2,1)S(1)} collective-permute-done((bf16[16,128,128]{2,1,0:T(8,128)(2,1)S(1)}, bf16[16,128,128]{2,1,0:T(8,128)(2,1)S(1)}, u32[]{:S(2)}, u32[]{:S(2)}) %collective-permute-start.19) | collective-permute-done | bytes 524320 | tf_op jit(solution)/shard_map/ppermute | solution.py:254
  122.1 2.4 %collective-permute-start.21 = (bf16[528,128]{1,0:T(8,128)(2,1)S(1)}, bf16[528,128]{1,0:T(8,128)(2,1)S(1)}, u32[]{:S(2)}, u32[]{:S(2)}) collective-permute-start(bf16[528,128]{1,0:T(8,128)(2,1)S(1)} %get-tuple-element.38), channel_id=1, source_target_pairs={{0,2},{1,3},{2,0},{3,1},{4,6},{5,7},{6,4},{7,5},{8,10},{9,11},{10,... | collective-permute-start | bytes 405512 | tf_op jit(solution)/shard_map/ppermute | solution.py:250
  125.1 3.3 %collective-permute-done.20.a = bf16[528,128]{1,0:T(8,128)(2,1)S(1)} collective-permute-done((bf16[528,128]{1,0:T(8,128)(2,1)S(1)}, bf16[528,128]{1,0:T(8,128)(2,1)S(1)}, u32[]{:S(2)}, u32[]{:S(2)}) %collective-permute-start.20) | collective-permute-done | bytes 135200 | tf_op jit(solution)/shard_map/ppermute | solution.py:250
  128.3 2.5 %collective-permute-done.21.b = bf16[528,128]{1,0:T(8,128)(2,1)S(1)} collective-permute-done((bf16[528,128]{1,0:T(8,128)(2,1)S(1)}, bf16[528,128]{1,0:T(8,128)(2,1)S(1)}, u32[]{:S(2)}, u32[]{:S(2)}) %collective-permute-start.21) | collective-permute-done | bytes 135200 | tf_op jit(solution)/shard_map/ppermute | solution.py:250
  (38 shorter events, 15.0 us)
Async XLA Ops:
  0.6 35.4 %copy-start.1 = (s32[1,1,1,256]{3,2,1,0:T(1,128)S(1)}, s32[1,1,1,256]{3,2,1,0:T(1,128)}, u32[]{:S(2)}) copy-start(s32[1,1,1,256]{3,2,1,0:T(1,128)} %param.7) | copy-start | bytes 3076
  6.5 4.9 %collective-permute-start = (bf16[16,128,128]{2,1,0:T(8,128)(2,1)S(1)}, bf16[16,128,128]{2,1,0:T(8,128)(2,1)S(1)}, u32[]{:S(2)}, u32[]{:S(2)}) collective-permute-start(bf16[16,128,128]{2,1,0:T(8,128)(2,1)S(1)} %get-tuple-element.24), channel_id=1, source_target_pairs={{0,128},{128,0},{1,129},{129,1},{2,130},{130,2},{3,131},{131,3},{4... | collective-permute-start | bytes 1572872 | tf_op jit(solution)/shard_map/ppermute | solution.py:254
  12.1 6.5 %collective-permute-start.1 = (bf16[4,128,128]{2,1,0:T(8,128)(2,1)S(1)}, bf16[4,128,128]{2,1,0:T(8,128)(2,1)S(1)}, u32[]{:S(2)}, u32[]{:S(2)}) collective-permute-start(bf16[4,128,128]{2,1,0:T(8,128)(2,1)S(1)} %get-tuple-element.26), channel_id=1, source_target_pairs={{0,1},{1,2},{2,3},{3,0},{4,5},{5,6},{6,7},{7,4},{8,9},{9,10},{10,1... | collective-permute-start | bytes 393224 | tf_op jit(solution)/shard_map/ppermute | solution.py:250
  12.2 8.3 %collective-permute-start.2 = (bf16[4,128,128]{2,1,0:T(8,128)(2,1)S(1)}, bf16[4,128,128]{2,1,0:T(8,128)(2,1)S(1)}, u32[]{:S(2)}, u32[]{:S(2)}) collective-permute-start(bf16[4,128,128]{2,1,0:T(8,128)(2,1)S(1)} %get-tuple-element.27), channel_id=1, source_target_pairs={{0,2},{1,3},{2,0},{3,1},{4,6},{5,7},{6,4},{7,5},{8,10},{9,11},{10,... | collective-permute-start | bytes 393224 | tf_op jit(solution)/shard_map/ppermute | solution.py:250
  14.3 6.8 %collective-permute-start.3 = (bf16[4,128,128]{2,1,0:T(8,128)(2,1)S(1)}, bf16[4,128,128]{2,1,0:T(8,128)(2,1)S(1)}, u32[]{:S(2)}, u32[]{:S(2)}) collective-permute-start(bf16[4,128,128]{2,1,0:T(8,128)(2,1)S(1)} %get-tuple-element.28), channel_id=1, source_target_pairs={{0,3},{1,0},{2,1},{3,2},{4,7},{5,4},{6,5},{7,6},{8,11},{9,8},{10,9... | collective-permute-start | bytes 393224 | tf_op jit(solution)/shard_map/ppermute | solution.py:250
  21.6 8.8 %collective-permute-start.6 = (bf16[4,128,128]{2,1,0:T(8,128)(2,1)S(1)}, bf16[4,128,128]{2,1,0:T(8,128)(2,1)S(1)}, u32[]{:S(2)}, u32[]{:S(2)}) collective-permute-start(bf16[4,128,128]{2,1,0:T(8,128)(2,1)S(1)} %first_sum.1.refs_0_), channel_id=1, source_target_pairs={{0,3},{1,0},{2,1},{3,2},{4,7},{5,4},{6,5},{7,6},{8,11},{9,8},{10,9... | collective-permute-start | bytes 393224 | tf_op jit(solution)/shard_map/ppermute | solution.py:250
  25.1 6.5 %collective-permute-start.5 = (bf16[4,128,128]{2,1,0:T(8,128)(2,1)S(1)}, bf16[4,128,128]{2,1,0:T(8,128)(2,1)S(1)}, u32[]{:S(2)}, u32[]{:S(2)}) collective-permute-start(bf16[4,128,128]{2,1,0:T(8,128)(2,1)S(1)} %first_sum.1.refs_0_), channel_id=1, source_target_pairs={{0,2},{1,3},{2,0},{3,1},{4,6},{5,7},{6,4},{7,5},{8,10},{9,11},{10,... | collective-permute-start | bytes 393224 | tf_op jit(solution)/shard_map/ppermute | solution.py:250
  25.1 9.1 %collective-permute-start.4 = (bf16[4,128,128]{2,1,0:T(8,128)(2,1)S(1)}, bf16[4,128,128]{2,1,0:T(8,128)(2,1)S(1)}, u32[]{:S(2)}, u32[]{:S(2)}) collective-permute-start(bf16[4,128,128]{2,1,0:T(8,128)(2,1)S(1)} %first_sum.1.refs_0_), channel_id=1, source_target_pairs={{0,1},{1,2},{2,3},{3,0},{4,5},{5,6},{6,7},{7,4},{8,9},{9,10},{10,1... | collective-permute-start | bytes 393224 | tf_op jit(solution)/shard_map/ppermute | solution.py:250
  25.8 9.3 %collective-permute-start.7 = (bf16[4,128,128]{2,1,0:T(8,128)(2,1)S(1)}, bf16[4,128,128]{2,1,0:T(8,128)(2,1)S(1)}, u32[]{:S(2)}, u32[]{:S(2)}) collective-permute-start(bf16[4,128,128]{2,1,0:T(8,128)(2,1)S(1)} %first_sum.1.refs_0_), channel_id=1, source_target_pairs={{0,128},{128,0},{1,129},{129,1},{2,130},{130,2},{3,131},{131,3},{4... | collective-permute-start | bytes 393224 | tf_op jit(solution)/shard_map/ppermute | solution.py:254
  30.4 4.6 %collective-permute-start.10 = (bf16[4,128,128]{2,1,0:T(8,128)(2,1)S(1)}, bf16[4,128,128]{2,1,0:T(8,128)(2,1)S(1)}, u32[]{:S(2)}, u32[]{:S(2)}) collective-permute-start(bf16[4,128,128]{2,1,0:T(8,128)(2,1)S(1)} %collective-permute-done.6.refs_3_), channel_id=1, source_target_pairs={{0,128},{128,0},{1,129},{129,1},{2,130},{130,2},{3,131},{131,3},{4... | collective-permute-start | bytes 393224 | tf_op jit(solution)/shard_map/ppermute | solution.py:254
  31.6 3.4 %collective-permute-start.9 = (bf16[4,128,128]{2,1,0:T(8,128)(2,1)S(1)}, bf16[4,128,128]{2,1,0:T(8,128)(2,1)S(1)}, u32[]{:S(2)}, u32[]{:S(2)}) collective-permute-start(bf16[4,128,128]{2,1,0:T(8,128)(2,1)S(1)} %collective-permute-done.5.refs_2_), channel_id=1, source_target_pairs={{0,128},{128,0},{1,129},{129,1},{2,130},{130,2},{3,131},{131,3},{4... | collective-permute-start | bytes 393224 | tf_op jit(solution)/shard_map/ppermute | solution.py:254
  34.2 1.8 %collective-permute-start.8 = (bf16[4,128,128]{2,1,0:T(8,128)(2,1)S(1)}, bf16[4,128,128]{2,1,0:T(8,128)(2,1)S(1)}, u32[]{:S(2)}, u32[]{:S(2)}) collective-permute-start(bf16[4,128,128]{2,1,0:T(8,128)(2,1)S(1)} %collective-permute-done.4.refs_1_), channel_id=1, source_target_pairs={{0,128},{128,0},{1,129},{129,1},{2,130},{130,2},{3,131},{131,3},{4... | collective-permute-start | bytes 393224 | tf_op jit(solution)/shard_map/ppermute | solution.py:254
  39.5 2.7 %collective-permute-start.11 = (bf16[32,128,128]{2,1,0:T(8,128)(2,1)S(1)}, bf16[32,128,128]{2,1,0:T(8,128)(2,1)S(1)}, u32[]{:S(2)}, u32[]{:S(2)}) collective-permute-start(bf16[32,128,128]{2,1,0:T(8,128)(2,1)S(1)} %get-tuple-element.30), channel_id=1, source_target_pairs={{0,128},{128,0},{1,129},{129,1},{2,130},{130,2},{3,131},{131,3},{4... | collective-permute-start | bytes 3145736 | tf_op jit(solution)/shard_map/ppermute | solution.py:254
  95.1 9.7 %collective-permute-start.14 = (bf16[8,128,128]{2,1,0:T(8,128)(2,1)S(1)}, bf16[8,128,128]{2,1,0:T(8,128)(2,1)S(1)}, u32[]{:S(2)}, u32[]{:S(2)}) collective-permute-start(bf16[8,128,128]{2,1,0:T(8,128)(2,1)S(1)} %all_to_all.11.refs_0_), channel_id=1, source_target_pairs={{0,96},{32,0},{64,32},{96,64},{1,97},{33,1},{65,33},{97,65},{2,98}... | collective-permute-start | bytes 786440 | tf_op jit(solution)/shard_map/ppermute | solution.py:250
  97.8 12.1 %collective-permute-start.13 = (bf16[8,128,128]{2,1,0:T(8,128)(2,1)S(1)}, bf16[8,128,128]{2,1,0:T(8,128)(2,1)S(1)}, u32[]{:S(2)}, u32[]{:S(2)}) collective-permute-start(bf16[8,128,128]{2,1,0:T(8,128)(2,1)S(1)} %all_to_all.11.refs_0_), channel_id=1, source_target_pairs={{0,64},{32,96},{64,0},{96,32},{1,65},{33,97},{65,1},{97,33},{2,66}... | collective-permute-start | bytes 786440 | tf_op jit(solution)/shard_map/ppermute | solution.py:250
  98.0 13.9 %collective-permute-start.12 = (bf16[8,128,128]{2,1,0:T(8,128)(2,1)S(1)}, bf16[8,128,128]{2,1,0:T(8,128)(2,1)S(1)}, u32[]{:S(2)}, u32[]{:S(2)}) collective-permute-start(bf16[8,128,128]{2,1,0:T(8,128)(2,1)S(1)} %all_to_all.11.refs_0_), channel_id=1, source_target_pairs={{0,32},{32,64},{64,96},{96,0},{1,33},{33,65},{65,97},{97,1},{2,34}... | collective-permute-start | bytes 786440 | tf_op jit(solution)/shard_map/ppermute | solution.py:250
  98.8 14.7 %collective-permute-start.15 = (bf16[8,128,128]{2,1,0:T(8,128)(2,1)S(1)}, bf16[8,128,128]{2,1,0:T(8,128)(2,1)S(1)}, u32[]{:S(2)}, u32[]{:S(2)}) collective-permute-start(bf16[8,128,128]{2,1,0:T(8,128)(2,1)S(1)} %all_to_all.11.refs_0_), channel_id=1, source_target_pairs={{0,128},{128,0},{1,129},{129,1},{2,130},{130,2},{3,131},{131,3},{4... | collective-permute-start | bytes 786440 | tf_op jit(solution)/shard_map/ppermute | solution.py:254
  104.8 8.7 %collective-permute-start.18 = (bf16[8,128,128]{2,1,0:T(8,128)(2,1)S(1)}, bf16[8,128,128]{2,1,0:T(8,128)(2,1)S(1)}, u32[]{:S(2)}, u32[]{:S(2)}) collective-permute-start(bf16[8,128,128]{2,1,0:T(8,128)(2,1)S(1)} %collective-permute-done.14.refs_3_), channel_id=1, source_target_pairs={{0,128},{128,0},{1,129},{129,1},{2,130},{130,2},{3,131},{131,3},{4... | collective-permute-start | bytes 786440 | tf_op jit(solution)/shard_map/ppermute | solution.py:254
  109.9 3.6 %collective-permute-start.17 = (bf16[8,128,128]{2,1,0:T(8,128)(2,1)S(1)}, bf16[8,128,128]{2,1,0:T(8,128)(2,1)S(1)}, u32[]{:S(2)}, u32[]{:S(2)}) collective-permute-start(bf16[8,128,128]{2,1,0:T(8,128)(2,1)S(1)} %collective-permute-done.13.refs_2_), channel_id=1, source_target_pairs={{0,128},{128,0},{1,129},{129,1},{2,130},{130,2},{3,131},{131,3},{4... | collective-permute-start | bytes 786440 | tf_op jit(solution)/shard_map/ppermute | solution.py:254
  111.9 2.8 %collective-permute-start.16 = (bf16[8,128,128]{2,1,0:T(8,128)(2,1)S(1)}, bf16[8,128,128]{2,1,0:T(8,128)(2,1)S(1)}, u32[]{:S(2)}, u32[]{:S(2)}) collective-permute-start(bf16[8,128,128]{2,1,0:T(8,128)(2,1)S(1)} %collective-permute-done.12.refs_1_), channel_id=1, source_target_pairs={{0,128},{128,0},{1,129},{129,1},{2,130},{130,2},{3,131},{131,3},{4... | collective-permute-start | bytes 786440 | tf_op jit(solution)/shard_map/ppermute | solution.py:254
  119.4 2.0 %collective-permute-start.19 = (bf16[16,128,128]{2,1,0:T(8,128)(2,1)S(1)}, bf16[16,128,128]{2,1,0:T(8,128)(2,1)S(1)}, u32[]{:S(2)}, u32[]{:S(2)}) collective-permute-start(bf16[16,128,128]{2,1,0:T(8,128)(2,1)S(1)} %get-tuple-element.33), channel_id=1, source_target_pairs={{0,128},{128,0},{1,129},{129,1},{2,130},{130,2},{3,131},{131,3},{4... | collective-permute-start | bytes 1572872 | tf_op jit(solution)/shard_map/ppermute | solution.py:254
  122.0 6.3 %collective-permute-start.20 = (bf16[528,128]{1,0:T(8,128)(2,1)S(1)}, bf16[528,128]{1,0:T(8,128)(2,1)S(1)}, u32[]{:S(2)}, u32[]{:S(2)}) collective-permute-start(bf16[528,128]{1,0:T(8,128)(2,1)S(1)} %get-tuple-element.37), channel_id=1, source_target_pairs={{0,1},{1,2},{2,3},{3,0},{4,5},{5,6},{6,7},{7,4},{8,9},{9,10},{10,1... | collective-permute-start | bytes 405512 | tf_op jit(solution)/shard_map/ppermute | solution.py:250
  122.1 8.7 %collective-permute-start.21 = (bf16[528,128]{1,0:T(8,128)(2,1)S(1)}, bf16[528,128]{1,0:T(8,128)(2,1)S(1)}, u32[]{:S(2)}, u32[]{:S(2)}) collective-permute-start(bf16[528,128]{1,0:T(8,128)(2,1)S(1)} %get-tuple-element.38), channel_id=1, source_target_pairs={{0,2},{1,3},{2,0},{3,1},{4,6},{5,7},{6,4},{7,5},{8,10},{9,11},{10,... | collective-permute-start | bytes 405512 | tf_op jit(solution)/shard_map/ppermute | solution.py:250
  124.6 6.8 %collective-permute-start.22 = (bf16[528,128]{1,0:T(8,128)(2,1)S(1)}, bf16[528,128]{1,0:T(8,128)(2,1)S(1)}, u32[]{:S(2)}, u32[]{:S(2)}) collective-permute-start(bf16[528,128]{1,0:T(8,128)(2,1)S(1)} %get-tuple-element.39), channel_id=1, source_target_pairs={{0,3},{1,0},{2,1},{3,2},{4,7},{5,4},{6,5},{7,6},{8,11},{9,8},{10,9... | collective-permute-start | bytes 405512 | tf_op jit(solution)/shard_map/ppermute | solution.py:250
  (1 other events, 35.4 us)
